TPU v7x, 32 devices: a whole 2x2x4 slice. The times are simulated.
32 devices in a mesh: wide: 16 (over z, x, core), narrow: 2 (over y).
Axes of the slice: x: 2, y: 2, z: 4, core: 2. Of those that a mesh axis runs over, the one named last changes fastest.
Arguments:
- frames: bfloat16 [32, 448, 768], P(('wide', 'narrow')), may hold values from -6 to 6
- dec_in: bfloat16 [32, 448, 768], P(('wide', 'narrow')), may hold values from -6 to 6
- cotangent: bfloat16 [32, 448, 768], P(('wide', 'narrow')), may hold values from -6 to 6
- dec_len: int32 [32], replicated, may hold values from 1 to 448, as said below
- bucket: int32 [32], replicated, may hold values from 0 to 3
- enc_weights: bfloat16 [9216, 768], P(('wide', 'narrow')), may hold values from -0.3247595 to 0.3247595
- enc_vectors: bfloat16 [9216], P(('wide', 'narrow')), may hold values from -0.75 to 1.46, as said below
- dec_weights: bfloat16 [12288, 768], P(('wide', 'narrow')), may hold values from -0.3247595 to 0.3247595
- dec_vectors: bfloat16 [13056], P(('wide', 'narrow')), may hold values from -0.75 to 1.46, as said below
Outputs:
- dec_out: bfloat16 [32, 448, 768], P(('wide', 'narrow'))
- d_dec_in: float32 [32, 448, 768], P(('wide', 'narrow'))
- d_enc: float32 [32, 448, 768], P(('wide', 'narrow'))
- d_dec_weights: float32 [12288, 768], P(('wide', 'narrow'))
- d_dec_vectors: float32 [13056], P(('wide', 'narrow'))
Inputs may be any that keep to these rules, and one draw needn't show every extreme that they name: `dec_len`: some item has exactly 448 tokens; most have few. `enc_vectors`: gains lie in 0.55 to 1.46, biases in -0.75 to 0.75. `dec_vectors`: gains lie in 0.55 to 1.46, biases in -0.75 to 0.75.
All inputs are finite; a program needn't handle non-finite values.
Results may differ from a plain program's by a relative error of at most 0.025.
Values may be sent and summed in bfloat16 or wider, within the bound.
No kernel may reach another device: no remote copies, remote signals or barrier semaphores. Data moves between devices by JAX's collectives and lax.ppermute only.
A program may use at most 192 MiB of HBM per device.

v0:
```python
import math

import jax
import jax.numpy as jnp
from jax import lax
from jax.sharding import PartitionSpec as P

D = 768
HEADS = 12
FF = 3072


EPS = 1e-05


def layer_norm(values, gain, bias):
    mean = jnp.mean(values, axis=-1, keepdims=True)
    centred = values - mean
    spread = jnp.mean(centred * centred, axis=-1, keepdims=True)
    return centred * lax.rsqrt(spread + EPS) * gain + bias


def activate(values):
    return jax.nn.gelu(values, approximate=False)


def times(left, right):
    return jnp.dot(left, right, preferred_element_type=jnp.float32)


def times_t(left, right):
    return lax.dot_general(
        left, right, (((1,), (1,)), ((), ())), preferred_element_type=jnp.float32
    )


def t_times(left, right):
    return lax.dot_general(
        left, right, (((0,), (0,)), ((), ())), preferred_element_type=jnp.float32
    )


def column_sums(values):
    return jnp.sum(values.astype(jnp.float32), axis=0)


def split_rows(stack, number):
    blocks = [stack[index * D : (index + 1) * D] for index in range(number)]
    return (blocks, stack[number * D : number * D + FF], stack[number * D + FF :])


def split_vector(vector, number):
    parts = [vector[index * D : (index + 1) * D].astype(jnp.float32) for index in range(number)]
    return (parts, vector[number * D :].astype(jnp.float32))


def by_heads(values):
    return values.reshape(values.shape[0], HEADS, D // HEADS)


def scores_of(query, keys, causal):
    scale = 1.0 / math.sqrt(D // HEADS)
    scores = (
        jnp.einsum(
            "qhd,khd->hqk", by_heads(query), by_heads(keys), preferred_element_type=jnp.float32
        )
        * scale
    )
    if causal:
        keep = jnp.arange(query.shape[0])[:, None] >= jnp.arange(keys.shape[0])[None, :]
        scores = jnp.where(keep[None], scores, -1e30)
    return scores


def attend(query, keys, values, causal):
    scores = scores_of(query, keys, causal)
    highest = jnp.max(scores, axis=-1, keepdims=True)
    weights = jnp.exp(scores - highest)
    totals = jnp.sum(weights, axis=-1, keepdims=True)
    probs = (weights / totals).astype(jnp.bfloat16)
    mixed = jnp.einsum("hqk,khd->qhd", probs, by_heads(values), preferred_element_type=jnp.float32)
    return (mixed.reshape(query.shape[0], D).astype(jnp.bfloat16), highest + jnp.log(totals))


def attend_back(query, keys, values, log_total, grad_mixed, causal):
    scale = 1.0 / math.sqrt(D // HEADS)
    probs = jnp.exp(scores_of(query, keys, causal) - log_total)
    grad_heads = by_heads(grad_mixed)
    grad_probs = jnp.einsum(
        "qhd,khd->hqk", grad_heads, by_heads(values), preferred_element_type=jnp.float32
    )
    grad_values = jnp.einsum(
        "hqk,qhd->khd", probs.astype(jnp.bfloat16), grad_heads, preferred_element_type=jnp.float32
    )
    grad_scores = (
        probs * (grad_probs - jnp.sum(grad_probs * probs, axis=-1, keepdims=True))
    ).astype(jnp.bfloat16)
    grad_query = (
        jnp.einsum("hqk,khd->qhd", grad_scores, by_heads(keys), preferred_element_type=jnp.float32)
        * scale
    )
    grad_keys = (
        jnp.einsum("hqk,qhd->khd", grad_scores, by_heads(query), preferred_element_type=jnp.float32)
        * scale
    )
    return (
        grad_query.reshape(query.shape[0], D).astype(jnp.bfloat16),
        grad_keys.reshape(keys.shape[0], D).astype(jnp.bfloat16),
        grad_values.reshape(keys.shape[0], D).astype(jnp.bfloat16),
    )


def norm_back(values, gain, bias, grad_normed):
    unused, backward = jax.vjp(layer_norm, values, gain, bias)
    return backward(grad_normed)


def encode(frame, stack, vector):
    (w_query, w_keys, w_values, w_output), up_weight, down_weight = split_rows(stack, 4)
    (
        gain_one,
        bias_one,
        gain_two,
        bias_two,
        bias_query,
        bias_values,
        bias_output,
        bias_down,
    ), bias_up = split_vector(vector, 8)
    inputs = frame.astype(jnp.float32)
    normed = layer_norm(inputs, gain_one, bias_one).astype(jnp.bfloat16)
    query = (times(normed, w_query) + bias_query).astype(jnp.bfloat16)
    keys = times(normed, w_keys).astype(jnp.bfloat16)
    values = (times(normed, w_values) + bias_values).astype(jnp.bfloat16)
    mixed, unused = attend(query, keys, values, False)
    after_attn = inputs + times(mixed, w_output) + bias_output
    normed_two = layer_norm(after_attn, gain_two, bias_two).astype(jnp.bfloat16)
    hidden = activate(times_t(normed_two, up_weight) + bias_up).astype(jnp.bfloat16)
    return (after_attn + times(hidden, down_weight) + bias_down).astype(jnp.bfloat16)


def rank_within(bucket_table):
    members = bucket_table.shape[-1]
    places = jnp.arange(members, dtype=jnp.int32)
    earlier = (bucket_table[:, None, :] < bucket_table[:, :, None]) | (
        bucket_table[:, None, :] == bucket_table[:, :, None]
    ) & (places[None, None, :] < places[None, :, None])
    return jnp.sum(earlier.astype(jnp.int32), axis=2)


def per_device(
    frames, dec_in, cotangent, dec_len, bucket, enc_weights, enc_vectors, dec_weights, dec_vectors
):
    members = lax.axis_size("narrow")
    wide_index = lax.axis_index("wide")
    narrow_index = lax.axis_index("narrow")
    enc_stack, enc_vector = (
        lax.all_gather(enc_weights, ("wide", "narrow"), axis=0, tiled=True),
        lax.all_gather(enc_vectors, ("wide", "narrow"), axis=0, tiled=True),
    )
    dec_stack, dec_vector = (
        lax.all_gather(dec_weights, ("wide", "narrow"), axis=0, tiled=True),
        lax.all_gather(dec_vectors, ("wide", "narrow"), axis=0, tiled=True),
    )
    encoded = encode(frames[0], enc_stack, enc_vector)
    frame_rows = encoded.shape[0]
    group_buckets = lax.dynamic_slice_in_dim(bucket, wide_index * members, members)
    group_lengths = lax.dynamic_slice_in_dim(dec_len, wide_index * members, members)
    rank_list = rank_within(group_buckets[None, :])[0]
    places = jnp.arange(members, dtype=jnp.int32)
    chosen = rank_list == narrow_index
    source = jnp.sum(jnp.where(chosen, places, 0))
    length = jnp.sum(jnp.where(chosen, group_lengths, 0))
    slice_rows = lax.all_gather(encoded, "narrow", axis=0, tiled=True)
    wanted = jnp.arange(frame_rows) + source * frame_rows
    inside = (wanted >= 0) & (wanted < slice_rows.shape[0])
    taken = jnp.take(slice_rows, jnp.clip(wanted, 0, slice_rows.shape[0] - 1), axis=0)
    memory = jnp.where(inside[:, None], taken, jnp.zeros_like(encoded))
    (self_q, self_k, self_v, self_o, cross_q, cross_k, cross_v, cross_o), up_weight, down_weight = (
        split_rows(dec_stack, 8)
    )
    (
        gain_one,
        bias_one,
        gain_two,
        bias_two,
        gain_three,
        bias_three,
        bias_sq,
        bias_sv,
        bias_so,
        bias_cq,
        bias_cv,
        bias_co,
        bias_down,
    ), bias_up = split_vector(dec_vector, 13)
    inputs = dec_in[0].astype(jnp.float32)
    live = (jnp.arange(inputs.shape[0]) < length)[:, None].astype(jnp.float32)
    normed_one = layer_norm(inputs, gain_one, bias_one).astype(jnp.bfloat16)
    query_self = (times(normed_one, self_q) + bias_sq).astype(jnp.bfloat16)
    keys_self = times(normed_one, self_k).astype(jnp.bfloat16)
    values_self = (times(normed_one, self_v) + bias_sv).astype(jnp.bfloat16)
    mixed_self, log_self = attend(query_self, keys_self, values_self, True)
    after_self = inputs + times(mixed_self, self_o) + bias_so
    normed_two = layer_norm(after_self, gain_two, bias_two).astype(jnp.bfloat16)
    query_cross = (times(normed_two, cross_q) + bias_cq).astype(jnp.bfloat16)
    keys_cross = times(memory, cross_k).astype(jnp.bfloat16)
    values_cross = (times(memory, cross_v) + bias_cv).astype(jnp.bfloat16)
    mixed_cross, log_cross = attend(query_cross, keys_cross, values_cross, False)
    after_cross = after_self + times(mixed_cross, cross_o) + bias_co
    normed_three = layer_norm(after_cross, gain_three, bias_three).astype(jnp.bfloat16)
    hidden_pre = times_t(normed_three, up_weight) + bias_up
    hidden = activate(hidden_pre).astype(jnp.bfloat16)
    result = after_cross + times(hidden, down_weight) + bias_down
    block_out = (live * result).astype(jnp.bfloat16)
    back_stack, back_vector = (
        lax.all_gather(dec_weights, ("wide", "narrow"), axis=0, tiled=True),
        lax.all_gather(dec_vectors, ("wide", "narrow"), axis=0, tiled=True),
    )
    (self_q, self_k, self_v, self_o, cross_q, cross_k, cross_v, cross_o), up_weight, down_weight = (
        split_rows(back_stack, 8)
    )
    (
        gain_one,
        bias_one,
        gain_two,
        bias_two,
        gain_three,
        bias_three,
        bias_sq,
        bias_sv,
        bias_so,
        bias_cq,
        bias_cv,
        bias_co,
        bias_down,
    ), bias_up = split_vector(back_vector, 13)
    grad_out = live * cotangent[0].astype(jnp.float32)
    round_down = grad_out.astype(jnp.bfloat16)
    grad_down = t_times(hidden, round_down)
    grad_bias_down = column_sums(round_down)
    unused, activate_back = jax.vjp(activate, hidden_pre)
    round_up = activate_back(times_t(round_down, down_weight))[0].astype(jnp.bfloat16)
    grad_up = t_times(round_up, normed_three)
    grad_bias_up = column_sums(round_up)
    grad_cross_in, grad_gain_three, grad_bias_three = norm_back(
        after_cross, gain_three, bias_three, times(round_up, up_weight)
    )
    grad_after_cross = grad_out + grad_cross_in
    round_cross = grad_after_cross.astype(jnp.bfloat16)
    grad_cross_o = t_times(mixed_cross, round_cross)
    grad_bias_co = column_sums(round_cross)
    grad_mixed_cross = times_t(round_cross, cross_o).astype(jnp.bfloat16)
    grad_query_cross, grad_keys_cross, grad_values_cross = attend_back(
        query_cross, keys_cross, values_cross, log_cross, grad_mixed_cross, False
    )
    grad_cross_q = t_times(normed_two, grad_query_cross)
    grad_bias_cq = column_sums(grad_query_cross)
    grad_cross_k = t_times(memory, grad_keys_cross)
    grad_cross_v = t_times(memory, grad_values_cross)
    grad_bias_cv = column_sums(grad_values_cross)
    grad_memory = times_t(grad_keys_cross, cross_k) + times_t(grad_values_cross, cross_v)
    grad_self_in, grad_gain_two, grad_bias_two = norm_back(
        after_self, gain_two, bias_two, times_t(grad_query_cross, cross_q)
    )
    grad_after_self = grad_after_cross + grad_self_in
    round_self = grad_after_self.astype(jnp.bfloat16)
    grad_self_o = t_times(mixed_self, round_self)
    grad_bias_so = column_sums(round_self)
    grad_mixed_self = times_t(round_self, self_o).astype(jnp.bfloat16)
    grad_query_self, grad_keys_self, grad_values_self = attend_back(
        query_self, keys_self, values_self, log_self, grad_mixed_self, True
    )
    grad_self_q = t_times(normed_one, grad_query_self)
    grad_bias_sq = column_sums(grad_query_self)
    grad_self_k = t_times(normed_one, grad_keys_self)
    grad_self_v = t_times(normed_one, grad_values_self)
    grad_bias_sv = column_sums(grad_values_self)
    grad_normed_one = (
        times_t(grad_query_self, self_q)
        + times_t(grad_keys_self, self_k)
        + times_t(grad_values_self, self_v)
    )
    grad_first_in, grad_gain_one, grad_bias_one = norm_back(
        inputs, gain_one, bias_one, grad_normed_one
    )
    grad_inputs = grad_after_self + grad_first_in
    grad_stack = jnp.concatenate(
        [
            grad_self_q,
            grad_self_k,
            grad_self_v,
            grad_self_o,
            grad_cross_q,
            grad_cross_k,
            grad_cross_v,
            grad_cross_o,
            grad_up,
            grad_down,
        ],
        axis=0,
    )
    grad_vector = jnp.concatenate(
        [
            grad_gain_one,
            grad_bias_one,
            grad_gain_two,
            grad_bias_two,
            grad_gain_three,
            grad_bias_three,
            grad_bias_sq,
            grad_bias_sv,
            grad_bias_so,
            grad_bias_cq,
            grad_bias_cv,
            grad_bias_co,
            grad_bias_down,
            grad_bias_up,
        ],
        axis=0,
    )
    shard_stack, shard_vector = (
        lax.psum_scatter(grad_stack, ("wide", "narrow"), scatter_dimension=0, tiled=True),
        lax.psum_scatter(grad_vector, ("wide", "narrow"), scatter_dimension=0, tiled=True),
    )
    wanted = jnp.arange(frame_rows * lax.axis_size("narrow")) - source * frame_rows
    inside = (wanted >= 0) & (wanted < frame_rows)
    taken = jnp.take(grad_memory, jnp.clip(wanted, 0, frame_rows - 1), axis=0)
    grad_encoded = lax.psum_scatter(
        jnp.where(inside[:, None], taken, 0.0).astype(jnp.bfloat16),
        "narrow",
        scatter_dimension=0,
        tiled=True,
    ).astype(jnp.float32)
    return (block_out[None], grad_inputs[None], grad_encoded[None], shard_stack, shard_vector)


def solution(mesh):
    placed = (
        P(("wide", "narrow"), None, None),
        P(("wide", "narrow"), None, None),
        P(("wide", "narrow"), None, None),
        P(),
        P(),
        P(("wide", "narrow"), None),
        P(("wide", "narrow")),
        P(("wide", "narrow"), None),
        P(("wide", "narrow")),
    )
    return jax.shard_map(
        per_device,
        mesh=mesh,
        in_specs=placed,
        out_specs=(
            P(("wide", "narrow"), None, None),
            P(("wide", "narrow"), None, None),
            P(("wide", "narrow"), None, None),
            P(("wide", "narrow"), None),
            P(("wide", "narrow")),
        ),
        check_vma=False,
    )
```

profile of v0, /device:TPU:0, one launch (start us, length us, event | category | flops | bytes accessed | tf_op | source)
XLA Modules:
  0.0 863.0 jit_solution(9388626416676729305)
XLA Ops:
  9.7 43.4 %all-reduce.3 = (bf16[13056]{0:T(1024)(128)(2,1)S(1)}, bf16[9216]{0:T(1024)(128)(2,1)S(1)}) all-reduce(bf16[13056]{0:T(1024)(128)(2,1)S(1)} %dynamic-update-slice, bf16[9216]{0:T(1024)(128)(2,1)S(1)} %dynamic-update-slice.1), channel_id=1, replica_groups=mesh['wide'=16,'narrow'=2] {'wide','narrow'}, use_global_device_ids=true, to_apply=%add | all-reduce | flops 22272 | bytes 89088
  55.9 61.8 %all-gather.6.cloned.1.call-done = bf16[9216,768]{1,0:T(8,128)(2,1)} async-done(((bf16[288,768]{1,0:T(8,128)(2,1)}), bf16[9216,768]{1,0:T(8,128)(2,1)}) %all-gather.6.cloned.1.call-update) | async-done | bytes 14155792 | tf_op jit(solution)/shard_map/all_gather | solution.py:158
  127.0 6.6 fusion.264
  133.6 5.2 fusion.116
  141.3 31.8 %fusion.146 = bf16[448,768]{1,0:T(8,128)(2,1)} fusion(f32[448,768]{1,0:T(8,128)S(1)} %get-tuple-element.56, bf16[9216,768]{1,0:T(8,128)(2,1)} %all-gather.6.cloned.1.call-done, f32[3072]{0:T(1024)S(1)} %slice_convert_fusion.1, f32[768]{0:T(1024)S(1)} %get-tuple-element.50, f32[768]{0:T(1024)S(1)} %get-tuple-element.44, f32[768]{0:T(1024)S(1)} %get-tuple-element.43, ...), kind=kOutput, calls=%fused_computation.214 | convolution fusion | flops 4321443840 | bytes 12906496 | tf_op jit(solution)/shard_map/dot_general | solution.py:28
  179.4 17.0 %all-gather.8.cloned.1.call-done = bf16[896,768]{1,0:T(8,128)(2,1)} async-done(((bf16[448,768]{1,0:T(8,128)(2,1)}), bf16[896,768]{1,0:T(8,128)(2,1)}) %all-gather.8.cloned.1.call-update) | async-done | bytes 1376272 | tf_op jit(solution)/shard_map/all_gather | solution.py:174
  196.4 4.6 gather_fusion
  201.0 123.1 %all-gather.4.cloned.1.call-done = bf16[12288,768]{1,0:T(8,128)(2,1)} async-done(((bf16[384,768]{1,0:T(8,128)(2,1)}), bf16[12288,768]{1,0:T(8,128)(2,1)}) %all-gather.4.cloned.1.call-update) | async-done | bytes 18874384 | tf_op jit(solution)/shard_map/all_gather | solution.py:162
  329.1 3.2 convolution_convert_fusion.4
  333.7 3.4 fusion.144
  339.4 3.1 convolution_convert_fusion.2
  351.0 3.5 fusion.115
  357.3 3.1 fusion.145
  373.0 17.8 %multiply_convert_fusion.2 = (bf16[448,3072]{1,0:T(8,128)(2,1)}, f32[448,3072]{1,0:T(8,128)S(1)}, f32[448,3072]{1,0:T(8,128)}) fusion(f32[3072]{0:T(1024)S(1)} %copy-done.73, bf16[12288,768]{1,0:T(8,128)(2,1)} %all-gather.4.cloned.1.call-done, f32[448,768]{1,0:T(8,128)S(1)} %get-tuple-element.62, f32[768]{0:T(1024)S(1)} %copy-done.82, ...), kind=kOutput, calls=%fused_computation.37 | convolution fusion | flops 2206482432 | bytes 19879424 | tf_op jit(solution)/shard_map/dot_general | solution.py:32
  390.7 8.5 convert_reduce_fusion
  399.2 6.5 multiply_reduce_fusion.4
  413.5 7.8 convert_reduce_fusion.3
  421.4 6.5 multiply_reduce_fusion.1
  427.9 4.4 multiply_convert_fusion.1
  436.7 3.4 multiply_reduce_fusion.5
  447.1 8.2 convert_reduce_fusion.5
  455.3 3.9 multiply_reduce_fusion
  459.2 3.8 multiply_convert_fusion
  471.9 3.8 gather_fusion.1
  477.4 3.7 convolution_dynamic-update-slice_fusion.9
  498.1 5.6 convolution_dynamic-update-slice_fusion.1
  503.7 5.3 convolution_dynamic-update-slice_fusion
  515.0 3.6 fusion.259
  521.7 38.8 %all-reduce.2 = f32[13056]{0:T(1024)S(1)} all-reduce(f32[13056]{0:T(1024)S(1)} %constant_dynamic-update-slice_fusion.10), channel_id=4, replica_groups=mesh['wide'=16,'narrow'=2] {'wide','narrow'}, use_global_device_ids=true, to_apply=%region_43.44.clone | all-reduce | flops 13056 | bytes 104448
  562.4 3.1 add_bitcast_fusion
  565.6 5.9 fusion.153
  573.8 282.5 %reduce-scatter.5.cloned.1.call-done = f32[384,768]{1,0:T(8,128)} async-done(((f32[12288,768]{1,0:T(8,128)}), f32[384,768]{1,0:T(8,128)}) %reduce-scatter.5.cloned.1.call-update) | async-done | bytes 1179664 | tf_op jit(solution)/shard_map/reduce_scatter | solution.py:323
  (345 shorter events, 114.2 us)
Async XLA Ops:
  7.2 110.5 %all-gather.6.cloned.1.call-start = ((), (), s32[]{:S(2)}) async-start(), calls=%async_computation.3 | async-start | bytes 14598144 | tf_op jit(solution)/shard_map/all_gather | solution.py:158
  7.9 188.5 %all-gather.8.cloned.1.call-start = ((), (), s32[]{:S(2)}) async-start(), calls=%async_computation.4 | async-start | bytes 2064384 | tf_op jit(solution)/shard_map/all_gather | solution.py:174
  141.2 32.6 %copy-start.93 = (s32[32]{0:T(128)S(1)}, s32[32]{0:T(128)}, u32[]{:S(2)}) copy-start(s32[32]{0:T(128)} %param.13) | copy-start | bytes 388
  141.3 32.9 %copy-start.92 = (s32[32]{0:T(128)S(1)}, s32[32]{0:T(128)}, u32[]{:S(2)}) copy-start(s32[32]{0:T(128)} %param.12) | copy-start | bytes 388
  141.3 36.3 %copy-start.10 = (bf16[1,448,768]{2,1,0:T(8,128)(2,1)S(1)}, bf16[1,448,768]{2,1,0:T(8,128)(2,1)}, u32[]{:S(2)}) copy-start(bf16[1,448,768]{2,1,0:T(8,128)(2,1)} %param.10) | copy-start | bytes 2064388
  173.1 151.0 %all-gather.4.cloned.1.call-start = ((), (), s32[]{:S(2)}) async-start(), calls=%async_computation.2 | async-start | bytes 19464192 | tf_op jit(solution)/shard_map/all_gather | solution.py:162
  173.8 397.7 %reduce-scatter.3.cloned.1.call-start = ((), (), s32[]{:S(2)}) async-start(), calls=%async_computation.5 | async-start | bytes 2064384 | tf_op jit(solution)/shard_map/reduce_scatter | solution.py:329
  175.6 163.8 %copy-start.96 = (pred[448]{0:T(512)(128)(4,1)}, pred[448]{0:T(512)(128)(4,1)S(1)}, u32[]{:S(2)}) copy-start(pred[448]{0:T(512)(128)(4,1)S(1)} %get-tuple-element.83) | copy-start | bytes 1348
  175.6 163.8 %copy-start.98 = (pred[448]{0:T(512)(128)(4,1)}, pred[448]{0:T(512)(128)(4,1)S(1)}, u32[]{:S(2)}) copy-start(pred[448]{0:T(512)(128)(4,1)S(1)} %get-tuple-element.84) | copy-start | bytes 1348
  176.9 263.9 %copy-start.56 = (f32[448]{0:T(512)}, f32[448]{0:T(512)S(1)}, u32[]{:S(2)}) copy-start(f32[448]{0:T(512)S(1)} %fusion.201) | copy-start | bytes 5380
  177.6 173.0 %copy-start.20 = (pred[448,448]{0,1:T(8,128)(4,1)}, pred[448,448]{0,1:T(8,128)(4,1)S(1)}, u32[]{:S(2)}) copy-start(pred[448,448]{0,1:T(8,128)(4,1)S(1)} %iota_compare_fusion) | copy-start | bytes 602116
  177.8 151.3 %copy-start.48 = (f32[448]{0:T(512)}, f32[448]{0:T(512)S(1)}, u32[]{:S(2)}) copy-start(f32[448]{0:T(512)S(1)} %broadcast_multiply_fusion.4) | copy-start | bytes 5380
  178.1 22.9 %copy-start.54 = (f32[448]{0:T(512)}, f32[448]{0:T(512)S(1)}, u32[]{:S(2)}) copy-start(f32[448]{0:T(512)S(1)} %fusion.130) | copy-start | bytes 5380
  178.1 151.0 %copy-start.59 = (f32[448]{0:T(512)}, f32[448]{0:T(512)S(1)}, u32[]{:S(2)}) copy-start(f32[448]{0:T(512)S(1)} %fusion.202) | copy-start | bytes 5380
  179.4 149.8 %copy-start.46 = (f32[768]{0:T(1024)}, f32[768]{0:T(1024)S(1)}, u32[]{:S(2)}) copy-start(f32[768]{0:T(1024)S(1)} %get-tuple-element.42) | copy-start | bytes 9220
  179.4 149.8 %copy-start.86 = (f32[768]{0:T(1024)}, f32[768]{0:T(1024)S(1)}, u32[]{:S(2)}) copy-start(f32[768]{0:T(1024)S(1)} %get-tuple-element.41) | copy-start | bytes 9220
  179.4 177.9 %copy-start.65 = (f32[768]{0:T(1024)}, f32[768]{0:T(1024)S(1)}, u32[]{:S(2)}) copy-start(f32[768]{0:T(1024)S(1)} %get-tuple-element.36) | copy-start | bytes 9220
  179.4 177.9 %copy-start.84 = (f32[768]{0:T(1024)}, f32[768]{0:T(1024)S(1)}, u32[]{:S(2)}) copy-start(f32[768]{0:T(1024)S(1)} %get-tuple-element.35) | copy-start | bytes 9220
  326.4 18.4 %copy-start.12 = (bf16[448,768]{0,1:T(8,128)(2,1)}, bf16[448,768]{0,1:T(8,128)(2,1)S(1)}, u32[]{:S(2)}) copy-start(bf16[448,768]{0,1:T(8,128)(2,1)S(1)} %copy.83) | copy-start | bytes 2064388
  329.1 21.4 %copy-start.22 = (bf16[448,768]{0,1:T(8,128)(2,1)}, bf16[448,768]{0,1:T(8,128)(2,1)S(1)}, u32[]{:S(2)}) copy-start(bf16[448,768]{0,1:T(8,128)(2,1)S(1)} %copy.82) | copy-start | bytes 2064388
  333.7 11.0 %copy-start.16 = (bf16[448,768]{0,1:T(8,128)(2,1)}, bf16[448,768]{0,1:T(8,128)(2,1)S(1)}, u32[]{:S(2)}) copy-start(bf16[448,768]{0,1:T(8,128)(2,1)S(1)} %copy.84) | copy-start | bytes 2064388
  356.9 83.2 %copy-start.4 = (f32[448,768]{1,0:T(8,128)}, f32[448,768]{1,0:T(8,128)S(1)}, u32[]{:S(2)}) copy-start(f32[448,768]{1,0:T(8,128)S(1)} %get-tuple-element.58) | copy-start | bytes 4128772
  372.6 33.2 %copy-start.2 = (f32[448,768]{1,0:T(8,128)}, f32[448,768]{1,0:T(8,128)S(1)}, u32[]{:S(2)}) copy-start(f32[448,768]{1,0:T(8,128)S(1)} %get-tuple-element.62) | copy-start | bytes 4128772
  372.6 33.2 %copy-start.52 = (f32[448]{0:T(512)}, f32[448]{0:T(512)S(1)}, u32[]{:S(2)}) copy-start(f32[448]{0:T(512)S(1)} %broadcast_multiply_fusion) | copy-start | bytes 5380
  372.9 32.9 %copy-start.77 = (f32[448]{0:T(512)}, f32[448]{0:T(512)S(1)}, u32[]{:S(2)}) copy-start(f32[448]{0:T(512)S(1)} %fusion.204) | copy-start | bytes 5380
  373.0 17.8 %copy-start.35 = (bf16[1,448,768]{2,1,0:T(8,128)(2,1)S(1)}, bf16[1,448,768]{2,1,0:T(8,128)(2,1)}, u32[]{:S(2)}) copy-start(bf16[1,448,768]{2,1,0:T(8,128)(2,1)} %param.11) | copy-start | bytes 2064388
  413.5 14.4 %slice-start = ((s8[11010048]{0:T(1024)(128)(4,1)}), s8[4194304]{0:T(1024)(128)(4,1)S(1)}, s32[]{:S(2)}) async-start(s8[11010048]{0:T(1024)(128)(4,1)} %bitcast.176), calls=%async_computation.7 | async-start | bytes 8388608
  413.5 14.4 %slice-start.1 = ((s8[11010048]{0:T(1024)(128)(4,1)}), s8[4194304]{0:T(1024)(128)(4,1)S(1)}, s32[]{:S(2)}) async-start(s8[11010048]{0:T(1024)(128)(4,1)} %bitcast.176), calls=%async_computation.8 | async-start | bytes 8388608
  443.7 11.6 %slice-start.3 = ((s8[11010048]{0:T(1024)(128)(4,1)}), s8[2621440]{0:T(1024)(128)(4,1)S(1)}, s32[]{:S(2)}) async-start(s8[11010048]{0:T(1024)(128)(4,1)} %bitcast.178), calls=%async_computation.10 | async-start | bytes 5242880
  447.0 8.3 copy-start.25
  447.0 8.3 copy-start.45
  477.3 379.0 %reduce-scatter.5.cloned.1.call-start = ((), (), s32[]{:S(2)}) async-start(), calls=%async_computation.6 | async-start | bytes 38928384 | tf_op jit(solution)/shard_map/reduce_scatter | solution.py:323
  (83 other events, 286.8 us)
Sparse Core Ops, SparseCore 0:
  10.9 106.6 all-gather.5
  173.2 23.1 all-gather.7
  199.3 124.6 all-gather.3
  477.4 22.0 reduce-scatter.2
  509.2 347.0 reduce-scatter.4
where the time goes:
time: 870 us; the launch traced here: 863 us
  waiting for transfers between devices  486 us (56%)
  matrix products  212 us (24%)
  blocking collectives  82.2 us (9%)
  other arithmetic  36.3 us (4%)
  local copies, waits for them, and re-layouts  30.9 us (4%)
  between operations  16.1 us (2%)
    reduce_scatter x1, waiting for transfers between devices, per_device(): lax.psum_scatter(grad_stack, ('wide', 'narrow'), scatter_dimension=0, til...  283 us
    all_gather x1, waiting for transfers between devices, per_device(): lax.all_gather(dec_weights, ('wide', 'narrow'), axis=0, tiled=True)  123 us
    unnamed x2, blocking collectives  82.2 us
    dot_general x15, matrix products, times(): return jnp.dot(left, right, preferred_element_type=jnp.float32)  75.9 us
    all_gather x1, waiting for transfers between devices, per_device(): lax.all_gather(enc_weights, ('wide', 'narrow'), axis=0, tiled=True)  61.8 us
    dot_general x10, matrix products, times_t(): lax.dot_general(left, right, (((1,), (1,)), ((), ())), preferred_element_...  47.5 us
    dot_general x10, matrix products, t_times(): lax.dot_general(left, right, (((0,), (0,)), ((), ())), preferred_element_...  31.4 us
  transfers between devices with their start and end apart: 5, of which 4 were waited for; matrix products, arithmetic and copies ran while one was open for 8% of the time, Pallas kernels for 0%

commit v1 on v0

v1 whole, which is shorter than its diff:
```python
import functools

import jax
import jax.numpy as jnp
from jax import lax
from jax.experimental import pallas as pl
from jax.experimental.pallas import tpu as pltpu
from jax.sharding import PartitionSpec as P

D = 768
HEADS = 12
FF = 3072
PAIR = 128
BLOCK = 384
SCALE = 0.125
EPS = 1e-05
F32 = jnp.float32
BF16 = jnp.bfloat16
VMEM_LIMIT = 56 * 1024 * 1024
ANY = pl.BlockSpec(memory_space=pl.ANY)
VMEM = pl.BlockSpec(memory_space=pltpu.VMEM)
SMEM = pl.BlockSpec(memory_space=pltpu.SMEM)


def mm(left, right):
    return jnp.dot(left, right, preferred_element_type=F32)


def mm_t(left, right):
    return lax.dot_general(left, right, (((1,), (1,)), ((), ())), preferred_element_type=F32)


def t_mm(left, right):
    return lax.dot_general(left, right, (((0,), (0,)), ((), ())), preferred_element_type=F32)


def normed(values):
    mean = jnp.mean(values, axis=-1, keepdims=True)
    centred = values - mean
    root = lax.rsqrt(jnp.mean(centred * centred, axis=-1, keepdims=True) + EPS)
    return centred * root, root


def norm_back(unit, root, gain, grad):
    scaled = grad * gain
    first = jnp.mean(scaled, axis=-1, keepdims=True)
    second = jnp.mean(scaled * unit, axis=-1, keepdims=True)
    return root * (scaled - first - unit * second)


def col_sum(values):
    return jnp.sum(values, axis=0, keepdims=True)


def lane_low(rows):
    return lax.broadcasted_iota(jnp.int32, (rows, PAIR), 1) < PAIR // 2


def attend(q_ref, k_ref, v_ref, o_ref, p_ref, causal):
    rows = q_ref.shape[0]
    keys = k_ref.shape[0]
    low = lane_low(rows)
    if causal:
        keep = lax.broadcasted_iota(jnp.int32, (rows, keys), 0) >= lax.broadcasted_iota(
            jnp.int32, (rows, keys), 1
        )

    def pair(index, carry):
        cols = pl.ds(pl.multiple_of(index * PAIR, PAIR), PAIR)
        query = q_ref[:, cols]
        key = k_ref[:, cols]
        value = v_ref[:, cols]
        halves = []
        for half in range(2):
            mine = low if half == 0 else jnp.logical_not(low)
            scores = mm_t(jnp.where(mine, query, jnp.zeros_like(query)), key) * SCALE
            if causal:
                scores = jnp.where(keep, scores, -1e30)
            weights = jnp.exp(scores - jnp.max(scores, axis=-1, keepdims=True))
            inverse = 1.0 / jnp.sum(weights, axis=-1, keepdims=True)
            probs = (weights * inverse).astype(BF16)
            if p_ref is not None:
                p_ref[index * 2 + half] = probs
            halves.append(mm(probs, value))
        o_ref[:, cols] = jnp.where(low, halves[0], halves[1]).astype(BF16)
        return carry

    lax.fori_loop(0, HEADS // 2, pair, 0)


def attend_back(q_ref, k_ref, v_ref, o_ref, do_ref, p_ref, dq_ref, dk_ref, dv_ref):
    rows = q_ref.shape[0]
    low = lane_low(rows)

    def pair(index, carry):
        cols = pl.ds(pl.multiple_of(index * PAIR, PAIR), PAIR)
        query = q_ref[:, cols]
        key = k_ref[:, cols]
        value = v_ref[:, cols]
        grad = do_ref[:, cols]
        both = grad.astype(F32) * o_ref[:, cols].astype(F32)
        d_query = jnp.zeros((rows, PAIR), F32)
        d_key = jnp.zeros((rows, PAIR), F32)
        d_value = jnp.zeros((rows, PAIR), F32)
        for half in range(2):
            mine = low if half == 0 else jnp.logical_not(low)
            zero = jnp.zeros_like(query)
            grad_half = jnp.where(mine, grad, zero)
            delta = jnp.sum(jnp.where(mine, both, 0.0), axis=-1, keepdims=True)
            probs = p_ref[index * 2 + half]
            d_probs = mm_t(grad_half, value)
            d_scores = (probs.astype(F32) * (d_probs - delta)).astype(BF16)
            d_value += t_mm(probs, grad_half)
            d_query += mm(d_scores, jnp.where(mine, key, zero))
            d_key += t_mm(d_scores, jnp.where(mine, query, zero))
        dq_ref[:, cols] = (d_query * SCALE).astype(BF16)
        dk_ref[:, cols] = (d_key * SCALE).astype(BF16)
        dv_ref[:, cols] = d_value.astype(BF16)
        return carry

    lax.fori_loop(0, HEADS // 2, pair, 0)


def gelu_parts(values):
    upper = 0.5 * (1.0 + lax.erf(values * 0.7071067811865476))
    slope = upper + values * (0.3989422804014327 * jnp.exp(-0.5 * values * values))
    return values * upper, slope


def piece_copies(offs_ref, piece_refs, stack_ref, sems):
    copies = []
    for index, piece in enumerate(piece_refs):
        start = pl.multiple_of(offs_ref[index], 16)
        copy = pltpu.make_async_copy(
            piece, stack_ref.at[pl.ds(start, piece.shape[0])], sems.at[index]
        )
        copy.start()
        copies.append(copy)
    return copies


def enc_one(n, offs_ref, x_ref, vec_ref, *refs):
    pieces, (o_ref, rest_ref, w_ref, q_ref, k_ref, v_ref, sems, out_sem) = refs[:n], refs[n:]
    copies = piece_copies(offs_ref, pieces, w_ref, sems)
    unit, unused = normed(x_ref[...].astype(F32))
    a = (unit * vec_ref[0:1] + vec_ref[1:2]).astype(BF16)
    for copy in copies:
        copy.wait()
    spill = pltpu.make_async_copy(w_ref.at[pl.ds(3 * D, rest_ref.shape[0])], rest_ref, out_sem)
    spill.start()
    q_ref[...] = (mm(a, w_ref[0:D]) + vec_ref[4:5]).astype(BF16)
    k_ref[...] = mm(a, w_ref[D : 2 * D]).astype(BF16)
    v_ref[...] = (mm(a, w_ref[2 * D : 3 * D]) + vec_ref[5:6]).astype(BF16)
    attend(q_ref, k_ref, v_ref, o_ref, None, False)
    spill.wait()


def enc_two(x_ref, o_ref, vec_ref, w_ref, e_ref, acc_ref, m_ref):
    x2 = x_ref[...].astype(F32) + mm(o_ref[...], w_ref[0:D]) + vec_ref[6:7]
    unit, unused = normed(x2)
    m_ref[...] = (unit * vec_ref[2:3] + vec_ref[3:4]).astype(BF16)
    acc_ref[...] = x2 + vec_ref[7:8]

    def tile(j, carry):
        base = pl.multiple_of(j * D, D)
        u = mm_t(m_ref[...], w_ref[pl.ds(D + base, D)]) + vec_ref[pl.ds(8 + j, 1)]
        hid = (u * (0.5 * (1.0 + lax.erf(u * 0.7071067811865476)))).astype(BF16)
        acc_ref[...] += mm(hid, w_ref[pl.ds(D + FF + base, D)])
        return carry

    lax.fori_loop(0, FF // D, tile, 0)
    e_ref[...] = acc_ref[...].astype(BF16)


def dec_one(n, offs_ref, x_ref, vec_ref, *refs):
    pieces = refs[:n]
    q_ref, k_ref, v_ref, o_ref, p_ref, x2_ref = refs[n : n + 6]
    outs = refs[n + 6 : n + 9]
    w_ref, sems, out_sems = refs[n + 9 :]
    copies = piece_copies(offs_ref, pieces, w_ref, sems)
    x = x_ref[...].astype(F32)
    unit, unused = normed(x)
    a = (unit * vec_ref[0:1] + vec_ref[1:2]).astype(BF16)
    for copy in copies:
        copy.wait()
    spills = []
    first = 0
    for index, out in enumerate(outs):
        spills.append(
            pltpu.make_async_copy(
                w_ref.at[pl.ds(first, out.shape[0])], out, out_sems.at[index]
            )
        )
        first += out.shape[0]
        spills[-1].start()
    q_ref[...] = (mm(a, w_ref[0:D]) + vec_ref[6:7]).astype(BF16)
    k_ref[...] = mm(a, w_ref[D : 2 * D]).astype(BF16)
    v_ref[...] = (mm(a, w_ref[2 * D : 3 * D]) + vec_ref[7:8]).astype(BF16)
    attend(q_ref, k_ref, v_ref, o_ref, p_ref, True)
    x2_ref[...] = x + mm(o_ref[...], w_ref[3 * D : 4 * D]) + vec_ref[8:9]
    for spill in spills:
        spill.wait()


def dec_two(flag_ref, x2_ref, mine_ref, other_ref, vec_ref, w_ref, *refs):
    e_ref, q_ref, k_ref, v_ref, o_ref, p_ref, x3_ref = refs
    x2 = x2_ref[...]
    unit, unused = normed(x2)
    a = (unit * vec_ref[2:3] + vec_ref[3:4]).astype(BF16)

    @pl.when(flag_ref[0] == 1)
    def same():
        e_ref[...] = mine_ref[...]

    @pl.when(flag_ref[0] != 1)
    def swapped():
        e_ref[...] = other_ref[...]

    e = e_ref[...]
    q_ref[...] = (mm(a, w_ref[0:D]) + vec_ref[9:10]).astype(BF16)
    k_ref[...] = mm(e, w_ref[D : 2 * D]).astype(BF16)
    v_ref[...] = (mm(e, w_ref[2 * D : 3 * D]) + vec_ref[10:11]).astype(BF16)
    attend(q_ref, k_ref, v_ref, o_ref, p_ref, False)
    x3_ref[...] = x2 + mm(o_ref[...], w_ref[3 * D : 4 * D]) + vec_ref[11:12]


class Emitter:
    def __init__(self, slot_ref, out_ref, stage_ref, sems):
        self.slot_ref, self.out_ref, self.stage_ref, self.sems = slot_ref, out_ref, stage_ref, sems
        self.pending = [None, None]
        self.turn = 0

    def copies(self, place, first_block):
        result = []
        for part in range(2):
            slot = self.slot_ref[first_block + part]
            result.append(
                pltpu.make_async_copy(
                    self.stage_ref.at[place, pl.ds(part * BLOCK, BLOCK)],
                    self.out_ref.at[slot],
                    self.sems.at[place, part],
                )
            )
        return result

    def put(self, first_block, value):
        place = self.turn % 2
        if self.pending[place] is not None:
            for copy in self.pending[place]:
                copy.wait()
        self.stage_ref[place] = value.astype(BF16)
        self.pending[place] = self.copies(place, first_block)
        for copy in self.pending[place]:
            copy.start()
        self.turn += 1

    def finish(self):
        for pending in self.pending:
            if pending is not None:
                for copy in pending:
                    copy.wait()


def dec_three(slot_ref, len_ref, x3_ref, cot_ref, vec_ref, w_ref, *refs):
    y_ref, dx_ref, gv_ref, gw_ref = refs[:4]
    a_ref, rm_ref, acc_ref, da_ref, stage_ref, sems = refs[4:]
    rows = x3_ref.shape[0]
    live = (lax.broadcasted_iota(jnp.int32, (rows, 1), 0) < len_ref[0]).astype(F32)
    unit, root = normed(x3_ref[...])
    a_ref[...] = (unit * vec_ref[4:5] + vec_ref[5:6]).astype(BF16)
    rm = (live * cot_ref[...].astype(F32)).astype(BF16)
    rm_ref[...] = rm
    gv_ref[2:3] = col_sum(rm.astype(F32))
    emit = Emitter(slot_ref, gw_ref, stage_ref, sems)
    for j in range(FF // D):
        up = w_ref[j * D : (j + 1) * D]
        down = w_ref[FF + j * D : FF + (j + 1) * D]
        u = mm_t(a_ref[...], up) + vec_ref[13 + j : 14 + j]
        hidden, slope = gelu_parts(u)
        hid = hidden.astype(BF16)
        part = mm(hid, down)
        du_wide = slope * mm_t(rm_ref[...], down)
        du = du_wide.astype(BF16)
        gv_ref[3 + j : 4 + j] = col_sum(du.astype(F32))
        emit.put(24 + 2 * j, t_mm(hid, rm_ref[...]))
        emit.put(16 + 2 * j, t_mm(du, a_ref[...]))
        back = mm(du, up)
        if j == 0:
            acc_ref[...] = part
            da_ref[...] = back
        else:
            acc_ref[...] += part
            da_ref[...] += back
    y_ref[...] = (live * (x3_ref[...] + acc_ref[...] + vec_ref[12:13])).astype(BF16)
    grad = da_ref[...]
    unit, root = normed(x3_ref[...])
    gv_ref[0:1] = col_sum(grad * unit)
    gv_ref[1:2] = col_sum(grad)
    dy = live * cot_ref[...].astype(F32)
    dx_ref[...] = dy + norm_back(unit, root, vec_ref[4:5], grad)
    emit.finish()


def dec_four(slot_ref, dx3_ref, x2_ref, e_ref, q_ref, k_ref, v_ref, o_ref, p_ref, vec_ref, w_ref, *refs):
    unused, dx_ref, de_ref, gv_ref, gw_ref = refs[:5]
    do_ref, dq_ref, dk_ref, dv_ref, stage_ref, sems = refs[5:]
    emit = Emitter(slot_ref, gw_ref, stage_ref, sems)
    rc = dx3_ref[...].astype(BF16)
    gv_ref[2:3] = col_sum(rc.astype(F32))
    do_ref[...] = mm_t(rc, w_ref[3 * D : 4 * D]).astype(BF16)
    emit.put(14, t_mm(o_ref[...], rc))
    attend_back(q_ref, k_ref, v_ref, o_ref, do_ref, p_ref, dq_ref, dk_ref, dv_ref)
    unit, root = normed(x2_ref[...])
    a = (unit * vec_ref[2:3] + vec_ref[3:4]).astype(BF16)
    dq = dq_ref[...]
    dk = dk_ref[...]
    dv = dv_ref[...]
    gv_ref[3:4] = col_sum(dq.astype(F32))
    gv_ref[4:5] = col_sum(dv.astype(F32))
    de_ref[...] = mm_t(dk, w_ref[D : 2 * D]) + mm_t(dv, w_ref[2 * D : 3 * D])
    emit.put(8, t_mm(a, dq))
    emit.put(10, t_mm(e_ref[...], dk))
    emit.put(12, t_mm(e_ref[...], dv))
    grad = mm_t(dq, w_ref[0:D])
    gv_ref[0:1] = col_sum(grad * unit)
    gv_ref[1:2] = col_sum(grad)
    dx_ref[...] = dx3_ref[...] + norm_back(unit, root, vec_ref[2:3], grad)
    emit.finish()


def dec_five(slot_ref, dx2_ref, x_ref, q_ref, k_ref, v_ref, o_ref, p_ref, vec_ref, w_ref, *refs):
    unused, dx_ref, gv_ref, gw_ref = refs[:4]
    do_ref, dq_ref, dk_ref, dv_ref, stage_ref, sems = refs[4:]
    emit = Emitter(slot_ref, gw_ref, stage_ref, sems)
    rs = dx2_ref[...].astype(BF16)
    gv_ref[2:3] = col_sum(rs.astype(F32))
    do_ref[...] = mm_t(rs, w_ref[3 * D : 4 * D]).astype(BF16)
    emit.put(6, t_mm(o_ref[...], rs))
    attend_back(q_ref, k_ref, v_ref, o_ref, do_ref, p_ref, dq_ref, dk_ref, dv_ref)
    unit, root = normed(x_ref[...].astype(F32))
    a = (unit * vec_ref[0:1] + vec_ref[1:2]).astype(BF16)
    dq = dq_ref[...]
    dk = dk_ref[...]
    dv = dv_ref[...]
    gv_ref[3:4] = col_sum(dq.astype(F32))
    gv_ref[4:5] = col_sum(dv.astype(F32))
    emit.put(0, t_mm(a, dq))
    emit.put(2, t_mm(a, dk))
    emit.put(4, t_mm(a, dv))
    grad = mm_t(dq, w_ref[0:D]) + mm_t(dk, w_ref[D : 2 * D]) + mm_t(dv, w_ref[2 * D : 3 * D])
    gv_ref[0:1] = col_sum(grad * unit)
    gv_ref[1:2] = col_sum(grad)
    dx_ref[...] = dx2_ref[...] + norm_back(unit, root, vec_ref[0:1], grad)
    emit.finish()


def shaped(shape, dtype):
    return jax.ShapeDtypeStruct(shape, dtype)


def call(body, out_shape, in_specs, out_specs, scratch, aliases=()):
    return pl.pallas_call(
        body,
        out_shape=out_shape,
        in_specs=in_specs,
        out_specs=out_specs,
        scratch_shapes=scratch,
        input_output_aliases=dict(aliases),
        compiler_params=pltpu.CompilerParams(vmem_limit_bytes=VMEM_LIMIT),
    )


def run_encoder(frame, vec, offs, pieces):
    rows = frame.shape[0]
    n = len(pieces)
    total = 4 * D + 2 * FF
    act = shaped((rows, D), BF16)
    o, rest = call(
        functools.partial(enc_one, n),
        (act, shaped((total - 3 * D, D), BF16)),
        [SMEM, VMEM, VMEM] + [ANY] * n,
        (VMEM, ANY),
        [pltpu.VMEM((total, D), BF16)]
        + [pltpu.VMEM((rows, D), BF16)] * 3
        + [pltpu.SemaphoreType.DMA((n,)), pltpu.SemaphoreType.DMA],
    )(offs, frame, vec, *pieces)
    return call(
        enc_two,
        act,
        [VMEM] * 4,
        VMEM,
        [pltpu.VMEM((rows, D), F32), pltpu.VMEM((rows, D), BF16)],
    )(frame, o, vec, rest)


def run_decoder(x, cot, mine, other, flag, length, vec, offs, pieces, slots):
    rows = x.shape[0]
    n = len(pieces)
    total = 8 * D + 2 * FF
    act = shaped((rows, D), BF16)
    wide = shaped((rows, D), F32)
    probs = shaped((HEADS, rows, rows), BF16)
    attn = shaped((4 * D, D), BF16)
    q1, k1, v1, o1, p1, x2, w_self, w_cross, w_ff = call(
        functools.partial(dec_one, n),
        (act, act, act, act, probs, wide, attn, attn, shaped((2 * FF, D), BF16)),
        [SMEM, VMEM, VMEM] + [ANY] * n,
        (VMEM,) * 6 + (ANY,) * 3,
        [
            pltpu.VMEM((total, D), BF16),
            pltpu.SemaphoreType.DMA((n,)),
            pltpu.SemaphoreType.DMA((3,)),
        ],
    )(offs, x, vec, *pieces)
    e, q2, k2, v2, o2, p2, x3 = call(
        dec_two,
        (act, act, act, act, act, probs, wide),
        [SMEM] + [VMEM] * 5,
        (VMEM,) * 7,
        [],
    )(flag, x2, mine, other, vec, w_cross)
    blocks = shaped((total // BLOCK, BLOCK, D), BF16)
    stage = [pltpu.VMEM((2, D, D), BF16), pltpu.SemaphoreType.DMA((2, 2))]
    act_v = pltpu.VMEM((rows, D), BF16)
    wide_v = pltpu.VMEM((rows, D), F32)
    y, dx3, gv3, gw = call(
        dec_three,
        (act, wide, shaped((7, D), F32), blocks),
        [SMEM, SMEM] + [VMEM] * 4,
        (VMEM, VMEM, VMEM, ANY),
        [act_v, act_v, wide_v, wide_v] + stage,
    )(slots, length, x3, cot, vec, w_ff)
    dx2, de, gv2, gw = call(
        dec_four,
        (wide, wide, shaped((5, D), F32), blocks),
        [SMEM] + [VMEM] * 10 + [ANY],
        (VMEM, VMEM, VMEM, ANY),
        [act_v] * 4 + stage,
        aliases=((11, 3),),
    )(slots, dx3, x2, e, q2, k2, v2, o2, p2, vec, w_cross, gw)
    dx, gv1, gw = call(
        dec_five,
        (wide, shaped((5, D), F32), blocks),
        [SMEM] + [VMEM] * 9 + [ANY],
        (VMEM, VMEM, ANY),
        [act_v] * 4 + stage,
        aliases=((10, 2),),
    )(slots, dx2, x, q1, k1, v1, o1, p1, vec, w_self, gw)
    vec_rows = jnp.concatenate(
        [
            gv1[0:2],
            gv2[0:2],
            gv3[0:2],
            gv1[3:5],
            gv1[2:3],
            gv2[3:5],
            gv2[2:3],
            gv3[2:7],
        ],
        axis=0,
    )
    return y, dx, de, gw, vec_rows


AXES = ("wide", "narrow")


class Grid:
    def __init__(self):
        wide = lax.axis_size("wide")
        self.fits = wide == 16 and lax.axis_size("narrow") == 2
        self.wide = wide
        self.w = lax.axis_index("wide")
        self.y = lax.axis_index("narrow")

    def shift(self, value, step):
        n = self.wide
        return lax.ppermute(value, "wide", [(i, (i + 4 * step) % n) for i in range(n)])

    def x_swap(self, value):
        return lax.ppermute(value, "wide", [(i, i ^ 2) for i in range(self.wide)])

    def core_swap(self, value):
        return lax.ppermute(value, "wide", [(i, i ^ 1) for i in range(self.wide)])

    def y_swap(self, value):
        return lax.ppermute(value, "narrow", [(0, 1), (1, 0)])

    def flat(self, k, dx, dc, dy):
        z = (self.w // 4 + 4 - k) % 4
        x = ((self.w // 2) % 2) ^ dx
        c = (self.w % 2) ^ dc
        return (((z * 2 + x) * 2 + c) * 2 + (self.y ^ dy)).astype(jnp.int32)


barrier = lax.optimization_barrier
ORDER = [
    (1, 1, 1),
    (2, 1, 1),
    (3, 1, 0),
    (3, 1, 1),
    (2, 1, 0),
    (2, 0, 1),
    (2, 0, 0),
    (0, 1, 1),
    (3, 0, 1),
    (3, 0, 0),
    (1, 1, 0),
    (1, 0, 1),
    (0, 0, 1),
    (1, 0, 0),
    (0, 1, 0),
    (0, 0, 0),
]


def gather(grid, shard):
    rows = shard.shape[0]
    if not grid.fits:
        return [lax.all_gather(shard, AXES, axis=0, tiled=True)], jnp.zeros((1,), jnp.int32)
    a0 = shard
    x0, y0, a1 = barrier((grid.x_swap(a0), grid.y_swap(a0), grid.shift(a0, 1)))
    d0, y1, a2 = barrier((grid.x_swap(y0), grid.y_swap(a1), grid.shift(a1, 1)))
    x1, y2, a3 = barrier((grid.x_swap(a1), grid.y_swap(a2), grid.shift(a2, 1)))
    x2, y3, d1 = barrier((grid.x_swap(a2), grid.y_swap(a3), grid.shift(d0, 1)))
    x3, d2, d3 = barrier((grid.x_swap(a3), grid.y_swap(x2), grid.shift(d0, -1)))
    found = [
        ((0, 0, 0), a0), ((0, 1, 0), x0), ((0, 0, 1), y0), ((1, 0, 0), a1),
        ((0, 1, 1), d0), ((1, 0, 1), y1), ((2, 0, 0), a2),
        ((1, 1, 0), x1), ((2, 0, 1), y2), ((3, 0, 0), a3),
        ((2, 1, 0), x2), ((3, 0, 1), y3), ((1, 1, 1), d1),
        ((3, 1, 0), x3), ((2, 1, 1), d2), ((3, 1, 1), d3),
    ]
    pieces = []
    starts = []
    for (k, dx, dy), piece in found:
        pieces.append(piece)
        starts.append(grid.flat(k, dx, 0, dy) * rows)
    for (k, dx, dy), piece in found:
        pieces.append(grid.core_swap(piece))
        starts.append(grid.flat(k, dx, 1, dy) * rows)
    return pieces, jnp.stack(starts)


def gather_vectors(grid, enc, dec):
    if not grid.fits:
        return (
            lax.all_gather(enc, AXES, axis=0, tiled=True),
            lax.all_gather(dec, AXES, axis=0, tiled=True),
        )
    size = enc.shape[0] + dec.shape[0]
    row = jnp.concatenate([enc, dec])[None]
    rows = jnp.concatenate([row, grid.core_swap(row)], axis=0)
    rows = jnp.concatenate([rows, grid.x_swap(rows)], axis=0)
    rows = jnp.concatenate([rows, grid.y_swap(rows)], axis=0)
    planes = [rows]
    for unused in range(3):
        planes.append(grid.shift(planes[-1], 1))
    rows = jnp.concatenate(planes, axis=0)
    where = jnp.stack(
        [
            grid.flat(k, dx, dc, dy)
            for k in range(4)
            for dy in range(2)
            for dx in range(2)
            for dc in range(2)
        ]
    )
    pick = (jnp.arange(where.shape[0])[:, None] == where[None, :]).astype(BF16)
    ordered = mm(pick, rows)
    return ordered[:, : enc.shape[0]].reshape(-1), ordered[:, enc.shape[0] : size].reshape(-1)


def slot_table(grid, blocks):
    if not grid.fits:
        return jnp.arange(blocks, dtype=jnp.int32)
    places = [
        (grid.flat(k, dx, dc, dy), dc * 16 + index)
        for dc in range(2)
        for index, (k, dx, dy) in enumerate(ORDER)
    ]
    where = jnp.stack([f for f, unused in places])
    values = jnp.array([s for unused, s in places], jnp.int32)
    return jnp.sum(
        jnp.where(jnp.arange(blocks)[:, None] == where[None, :], values[None, :], 0), axis=1
    ).astype(jnp.int32)


def reduce_weights(grid, gw):
    if not grid.fits:
        return lax.psum_scatter(
            gw.reshape(-1, D), AXES, scatter_dimension=0, tiled=True
        ).astype(F32)
    came = []
    for part in range(4):
        came.append(grid.core_swap(gw[16 + 4 * part : 20 + 4 * part]))

    def term(k, dx, dy):
        index = ORDER.index((k, dx, dy))
        return gw[index].astype(F32) + came[index // 4][index % 4].astype(F32)

    def low(value):
        return value.astype(BF16)

    def up(value):
        return value.astype(F32)

    def total(key, *more):
        value = term(*key)
        for one in more:
            value = value + up(one)
        return value

    d1, d2, x3 = barrier(
        (
            grid.shift(low(total((1, 1, 1))), -1),
            grid.y_swap(low(total((2, 1, 1)))),
            grid.x_swap(low(total((3, 1, 0)))),
        )
    )
    d3, x2, y2 = barrier(
        (
            grid.shift(low(total((3, 1, 1))), 1),
            grid.x_swap(low(total((2, 1, 0), d2))),
            grid.y_swap(low(total((2, 0, 1)))),
        )
    )
    a2, d0, y3 = barrier(
        (
            grid.shift(low(total((2, 0, 0), x2, y2)), -1),
            grid.x_swap(low(total((0, 1, 1), d1, d3))),
            grid.y_swap(low(total((3, 0, 1)))),
        )
    )
    a3, x1, y1 = barrier(
        (
            grid.shift(low(total((3, 0, 0), x3, y3)), 1),
            grid.x_swap(low(total((1, 1, 0)))),
            grid.y_swap(low(total((1, 0, 1)))),
        )
    )
    a1, x0, y0 = barrier(
        (
            grid.shift(low(total((1, 0, 0), a2, x1, y1)), -1),
            grid.x_swap(low(total((0, 1, 0)))),
            grid.y_swap(low(total((0, 0, 1), d0))),
        )
    )
    return total((0, 0, 0), a1, a3, x0, y0)


def reduce_vectors(grid, rows):
    if not grid.fits:
        return lax.psum_scatter(rows.reshape(-1), AXES, scatter_dimension=0, tiled=True)
    rows = rows + grid.core_swap(rows)
    rows = rows + grid.x_swap(rows)
    rows = rows + grid.y_swap(rows)
    rows = rows + grid.shift(rows, 1)
    rows = rows + grid.shift(rows, 2)
    flat = rows.reshape(-1)
    size = flat.shape[0] // (grid.wide * 2)
    return lax.dynamic_slice_in_dim(flat, grid.flat(0, 0, 0, 0) * size, size)


def rank_within(buckets):
    places = jnp.arange(buckets.shape[0], dtype=jnp.int32)
    earlier = (buckets[None, :] < buckets[:, None]) | (
        (buckets[None, :] == buckets[:, None]) & (places[None, :] < places[:, None])
    )
    return jnp.sum(earlier.astype(jnp.int32), axis=1)


def per_device(
    frames, dec_in, cotangent, dec_len, bucket, enc_weights, enc_vectors, dec_weights, dec_vectors
):
    grid = Grid()
    members = lax.axis_size("narrow")
    wide_index = lax.axis_index("wide")
    narrow_index = lax.axis_index("narrow")
    group_buckets = lax.dynamic_slice_in_dim(bucket, wide_index * members, members)
    group_lengths = lax.dynamic_slice_in_dim(dec_len, wide_index * members, members)
    ranks = rank_within(group_buckets)
    places = jnp.arange(members, dtype=jnp.int32)
    chosen = ranks == narrow_index
    source = jnp.sum(jnp.where(chosen, places, 0))
    length = jnp.sum(jnp.where(chosen, group_lengths, 0))
    own_slot = jnp.sum(jnp.where(places == narrow_index, ranks, 0))

    enc_vec, dec_vec = gather_vectors(grid, enc_vectors, dec_vectors)
    enc_vec = enc_vec.astype(F32).reshape(-1, D)
    dec_vec = dec_vec.astype(F32).reshape(-1, D)
    enc_pieces, enc_offs = gather(grid, enc_weights)
    if grid.fits:
        dec_weights, enc_pieces = barrier((dec_weights, enc_pieces))
    dec_pieces, dec_offs = gather(grid, dec_weights)
    encoded = run_encoder(frames[0], enc_vec, enc_offs, enc_pieces)
    if members == 2:
        other = grid.y_swap(encoded)
    else:
        every = lax.all_gather(encoded, "narrow", axis=0)
        other = lax.dynamic_index_in_dim(every, source, keepdims=False)
    flag = (source == narrow_index).astype(jnp.int32)[None]
    slots = slot_table(grid, (8 * D + 2 * FF) // BLOCK)
    block_out, grad_inputs, grad_memory, grad_blocks, grad_rows = run_decoder(
        dec_in[0],
        cotangent[0],
        encoded,
        other,
        flag,
        length[None],
        dec_vec,
        dec_offs,
        dec_pieces,
        slots,
    )
    if members == 2:
        back = grid.y_swap(grad_memory.astype(BF16)).astype(F32)
    else:
        every = lax.all_gather(grad_memory.astype(BF16), "narrow", axis=0)
        back = lax.dynamic_index_in_dim(every, own_slot, keepdims=False).astype(F32)
    grad_encoded = jnp.where(own_slot == narrow_index, grad_memory, back)
    shard_stack = reduce_weights(grid, grad_blocks)
    shard_vector = reduce_vectors(grid, grad_rows)
    return (block_out[None], grad_inputs[None], grad_encoded[None], shard_stack, shard_vector)


def solution(mesh):
    items = P(AXES, None, None)
    rows = P(AXES, None)
    line = P(AXES)
    return jax.shard_map(
        per_device,
        mesh=mesh,
        in_specs=(items, items, items, P(), P(), rows, line, rows, line),
        out_specs=(items, items, items, rows, line),
        check_vma=False,
    )
```

time: 870 us -> 468 us (0.54)
  waiting for transfers between devices: 486 us -> 230 us
  matrix products: 212 us -> 0.13 us
  Pallas kernels: 0 us -> 136 us
  blocking collectives: 82.2 us -> 0 us
  starting transfers between devices: 0.2 us -> 64.7 us
  local copies, waits for them, and re-layouts: 30.9 us -> 10.5 us
  other arithmetic: 36.3 us -> 18.7 us
  between operations: 16.1 us -> 3 us
    reduce_scatter x2 -> x0, waiting for transfers between devices: 283 us -> none  [the longest x1 283 us: per_device(): lax.psum_scatter(grad_stack, ('wide', 'narrow'), scatter_dimension=0, til...]
    ppermute x0 -> x94, waiting for transfers between devices: none -> 230 us  [the longest x20 95 us: shift(): lax.ppermute(value, 'wide', [(i, (i + 4 * step) % n) for i in range(n)])]
    dot_general x48 -> x1, matrix products: 205 us -> 0.13 us  [mm(): return jnp.dot(left, right, preferred_element_type=F32)]
    all_gather x3 -> x0, waiting for transfers between devices: 202 us -> none  [the longest x1 123 us: per_device(): lax.all_gather(dec_weights, ('wide', 'narrow'), axis=0, tiled=True)]
    pallas_call x0 -> x7, Pallas kernels: none -> 136 us  [the longest x1 25.5 us: run_decoder(): call(dec_three, (act, wide, shaped((7, D), F32), blocks), [SMEM, SMEM] +...]
    unnamed x2 -> x0, blocking collectives: 82.2 us -> none
    ppermute x0 -> x94, starting transfers between devices: none -> 64.7 us  [the longest x17 19.4 us: x_swap(): return lax.ppermute(value, 'wide', [(i, i ^ 2) for i in range(self.wide)])]
    reduce_sum x16 -> x3, other arithmetic: 15.3 us -> 1.6 us  [the longest x1 0.79 us: per_device(): own_slot = jnp.sum(jnp.where(places == narrow_index, ranks, 0))]
  transfers between devices with their start and end apart: 5 -> 94, of which waited for: 4 -> 52; matrix products, arithmetic and copies ran while one was open for 8% -> 4% of each run, Pallas kernels for 0% -> 11%
where the time goes in v1:
time: 468 us; the launch traced here: 464 us
  waiting for transfers between devices  230 us (49%)
  Pallas kernels  136 us (29%)
  starting transfers between devices  64.7 us (14%)
  other arithmetic  18.7 us (4%)
  local copies, waits for them, and re-layouts  10.5 us (2%)
    ppermute x20, waiting for transfers between devices, shift(): lax.ppermute(value, 'wide', [(i, (i + 4 * step) % n) for i in range(n)])  95 us
    ppermute x17, waiting for transfers between devices, x_swap(): return lax.ppermute(value, 'wide', [(i, i ^ 2) for i in range(self.wide)])  90.9 us
    pallas_call x1, Pallas kernels, run_decoder(): call(dec_three, (act, wide, shaped((7, D), F32), blocks), [SMEM, SMEM] +...  25.5 us
    ppermute x19, waiting for transfers between devices, y_swap(): return lax.ppermute(value, 'narrow', [(0, 1), (1, 0)])  24.5 us
    pallas_call x1, Pallas kernels, run_decoder(): call(dec_five, (wide, shaped((5, D), F32), blocks), [SMEM] + [VMEM] * 9 +...  22.8 us
    pallas_call x1, Pallas kernels, run_decoder(): call(dec_four, (wide, wide, shaped((5, D), F32), blocks), [SMEM] + [VMEM]...  22.4 us
    pallas_call x1, Pallas kernels, run_decoder(): call(functools.partial(dec_one, n), (act, act, act, act, probs, wide, att...  20.9 us
    ppermute x38, waiting for transfers between devices, core_swap(): return lax.ppermute(value, 'wide', [(i, i ^ 1) for i in range(self.wide)])  19.9 us
  transfers between devices with their start and end apart: 94, of which 52 were waited for; matrix products, arithmetic and copies ran while one was open for 4% of the time, Pallas kernels for 11%

profile of v1, /device:TPU:0, one launch (start us, length us, event | category | flops | bytes accessed | tf_op | source)
XLA Modules:
  0.0 463.6 jit_solution(3158867281530242545)
XLA Ops:
  6.7 7.3 %collective-permute-done.6.refs_1_ = bf16[288,768]{1,0:T(8,128)(2,1)S(1)} collective-permute-done((bf16[288,768]{1,0:T(8,128)(2,1)}, bf16[288,768]{1,0:T(8,128)(2,1)S(1)}, u32[]{:S(2)}, u32[]{:S(2)}) %collective-permute-start.6) | collective-permute-done | bytes 442400 | tf_op jit(solution)/shard_map/ppermute | solution.py:481
  21.1 8.0 %collective-permute-done.10.refs_5_ = bf16[288,768]{1,0:T(8,128)(2,1)S(1)} collective-permute-done((bf16[288,768]{1,0:T(8,128)(2,1)S(1)}, bf16[288,768]{1,0:T(8,128)(2,1)S(1)}, u32[]{:S(2)}, u32[]{:S(2)}) %collective-permute-start.10) | collective-permute-done | bytes 442400 | tf_op jit(solution)/shard_map/ppermute | solution.py:487
  41.8 4.7 %collective-permute-done.14.refs_9_ = bf16[288,768]{1,0:T(8,128)(2,1)S(1)} collective-permute-done((bf16[288,768]{1,0:T(8,128)(2,1)S(1)}, bf16[288,768]{1,0:T(8,128)(2,1)S(1)}, u32[]{:S(2)}, u32[]{:S(2)}) %collective-permute-start.14) | collective-permute-done | bytes 442400 | tf_op jit(solution)/shard_map/ppermute | solution.py:478
  51.9 3.8 collective-permute-done.17.refs_12_
  57.4 5.4 %collective-permute-done.20.refs_15_ = bf16[288,768]{1,0:T(8,128)(2,1)S(1)} collective-permute-done((bf16[288,768]{1,0:T(8,128)(2,1)S(1)}, bf16[288,768]{1,0:T(8,128)(2,1)S(1)}, u32[]{:S(2)}, u32[]{:S(2)}) %collective-permute-start.20) | collective-permute-done | bytes 442400 | tf_op jit(solution)/shard_map/ppermute | solution.py:478
  63.4 5.0 %collective-permute-done.18.refs_13_ = bf16[288,768]{1,0:T(8,128)(2,1)S(1)} collective-permute-done((bf16[288,768]{1,0:T(8,128)(2,1)S(1)}, bf16[288,768]{1,0:T(8,128)(2,1)S(1)}, u32[]{:S(2)}, u32[]{:S(2)}) %collective-permute-start.18) | collective-permute-done | bytes 442400 | tf_op jit(solution)/shard_map/ppermute | solution.py:481
  75.5 14.4 %collective-permute-done.37.refs_1_ = bf16[384,768]{1,0:T(8,128)(2,1)S(1)} collective-permute-done((bf16[384,768]{1,0:T(8,128)(2,1)}, bf16[384,768]{1,0:T(8,128)(2,1)S(1)}, u32[]{:S(2)}, u32[]{:S(2)}) %collective-permute-start.37) | collective-permute-done | bytes 589856 | tf_op jit(solution)/shard_map/ppermute | solution.py:481
  90.5 7.4 %collective-permute-done.39.refs_3_ = bf16[384,768]{1,0:T(8,128)(2,1)S(1)} collective-permute-done((bf16[384,768]{1,0:T(8,128)(2,1)}, bf16[384,768]{1,0:T(8,128)(2,1)S(1)}, u32[]{:S(2)}, u32[]{:S(2)}) %collective-permute-start.39) | collective-permute-done | bytes 589856 | tf_op jit(solution)/shard_map/ppermute | solution.py:478
  105.0 20.0 %collective-permute-done.1 = bf16[2,696]{1,0:T(2,128)(2,1)S(1)} collective-permute-done((bf16[2,696]{1,0:T(2,128)(2,1)S(1)}, bf16[2,696]{1,0:T(2,128)(2,1)S(1)}, u32[]{:S(2)}, u32[]{:S(2)}) %collective-permute-start.1) | collective-permute-done | bytes 2816 | tf_op jit(solution)/shard_map/ppermute | solution.py:481
  129.6 5.0 %collective-permute-done.3 = bf16[8,696]{1,0:T(8,128)(2,1)S(1)} collective-permute-done((bf16[8,696]{1,0:T(8,128)(2,1)S(1)}, bf16[8,696]{1,0:T(8,128)(2,1)S(1)}, u32[]{:S(2)}, u32[]{:S(2)}) %collective-permute-start.3) | collective-permute-done | bytes 11168 | tf_op jit(solution)/shard_map/ppermute | solution.py:478
  134.6 8.7 %collective-permute-done.4 = bf16[8,696]{1,0:T(8,128)(2,1)S(1)} collective-permute-done((bf16[8,696]{1,0:T(8,128)(2,1)S(1)}, bf16[8,696]{1,0:T(8,128)(2,1)S(1)}, u32[]{:S(2)}, u32[]{:S(2)}) %collective-permute-start.4) | collective-permute-done | bytes 11168 | tf_op jit(solution)/shard_map/ppermute | solution.py:478
  143.9 5.5 %collective-permute-done.5 = bf16[8,696]{1,0:T(8,128)(2,1)S(1)} collective-permute-done((bf16[8,696]{1,0:T(8,128)(2,1)S(1)}, bf16[8,696]{1,0:T(8,128)(2,1)S(1)}, u32[]{:S(2)}, u32[]{:S(2)}) %collective-permute-start.5) | collective-permute-done | bytes 11168 | tf_op jit(solution)/shard_map/ppermute | solution.py:478
  150.7 4.0 collective-permute-start.51
  156.0 8.1 %collective-permute-done.46.refs_10_ = bf16[384,768]{1,0:T(8,128)(2,1)} collective-permute-done((bf16[384,768]{1,0:T(8,128)(2,1)S(1)}, bf16[384,768]{1,0:T(8,128)(2,1)}, u32[]{:S(2)}, u32[]{:S(2)}) %collective-permute-start.46) | collective-permute-done | bytes 589856 | tf_op jit(solution)/shard_map/ppermute | solution.py:481
  164.0 4.7 %collective-permute-done.48.refs_12_ = bf16[384,768]{1,0:T(8,128)(2,1)S(1)} collective-permute-done((bf16[384,768]{1,0:T(8,128)(2,1)S(1)}, bf16[384,768]{1,0:T(8,128)(2,1)S(1)}, u32[]{:S(2)}, u32[]{:S(2)}) %collective-permute-start.48) | collective-permute-done | bytes 589856 | tf_op jit(solution)/shard_map/ppermute | solution.py:478
  168.7 9.1 %collective-permute-done.51.refs_15_ = bf16[384,768]{1,0:T(8,128)(2,1)S(1)} collective-permute-done((bf16[384,768]{1,0:T(8,128)(2,1)S(1)}, bf16[384,768]{1,0:T(8,128)(2,1)S(1)}, u32[]{:S(2)}, u32[]{:S(2)}) %collective-permute-start.51) | collective-permute-done | bytes 589856 | tf_op jit(solution)/shard_map/ppermute | solution.py:478
  181.0 10.6 %collective-permute-done.49.refs_13_ = bf16[384,768]{1,0:T(8,128)(2,1)S(1)} collective-permute-done((bf16[384,768]{1,0:T(8,128)(2,1)}, bf16[384,768]{1,0:T(8,128)(2,1)S(1)}, u32[]{:S(2)}, u32[]{:S(2)}) %collective-permute-start.49) | collective-permute-done | bytes 589856 | tf_op jit(solution)/shard_map/ppermute | solution.py:481
  194.4 16.5 %shard_map.138 = (bf16[448,768]{1,0:T(8,128)(2,1)}, bf16[6912,768]{1,0:T(8,128)(2,1)}) custom-call(s32[32]{0:T(128)} %stack.431.offs_ref, bf16[448,768]{1,0:T(8,128)(2,1)} %bitcast.166, f32[12,768]{1,0:T(8,128)} %reshape_reshape.7.vec_ref, bf16[288,768]{1,0:T(8,128)(2,1)} %refs_0_.1, bf16[288,768]{1,0:T(8,128)(2,1)} %copy-done.25, ...), custom_call_target="tpu_custom_call" | custom-call | tf_op jit(solution)/shard_map/pallas_call | solution.py:378
  210.9 12.3 %shard_map.139.mine_ref = bf16[448,768]{1,0:T(8,128)(2,1)} custom-call(bf16[448,768]{1,0:T(8,128)(2,1)} %bitcast.167, bf16[448,768]{1,0:T(8,128)(2,1)} %get-tuple-element.176.o_ref, f32[12,768]{1,0:T(8,128)} %reshape_reshape.7.vec_ref, bf16[6912,768]{1,0:T(8,128)(2,1)} %get-tuple-element.177.w_ref), custom_call_target="tpu_custom_call" | custom-call | tf_op jit(solution)/shard_map/pallas_call | solution.py:387
  230.4 20.9 %shard_map.137 = (bf16[448,768]{1,0:T(8,128)(2,1)}, bf16[448,768]{1,0:T(8,128)(2,1)}, bf16[448,768]{1,0:T(8,128)(2,1)}, bf16[448,768]{1,0:T(8,128)(2,1)}, bf16[1...) custom-call(s32[32]{0:T(128)} %stack.397.offs_ref, ...), custom_call_target="tpu_custom_call" | custom-call | tf_op jit(solution)/shard_map/pallas_call | solution.py:404
  252.1 15.9 %shard_map.140 = (bf16[448,768]{1,0:T(8,128)(2,1)}, bf16[448,768]{1,0:T(8,128)(2,1)}, bf16[448,768]{1,0:T(8,128)(2,1)}, bf16[448,768]{1,0:T(8,128)(2,1)}, bf16[4...) custom-call(s32[1]{0:T(128)} %bitcast.33.flag_ref, f32[448,768]{1,0:T(8,128)} %get-tuple-element.143.x2_ref, ...), custom_call_target="tpu_custom_call" | custom-call | tf_op jit(solution)/shard_map/pallas_call | solution.py:415
  268.0 25.5 %shard_map.141 = (bf16[448,768]{1,0:T(8,128)(2,1)}, f32[448,768]{1,0:T(8,128)}, f32[7,768]{1,0:T(8,128)}, bf16[32,384,768]{2,1,0:T(8,128)(2,1)}) custom-call(s32[32]{0:T(128)} %fusion.23.slot_ref, s32[1]{0:T(128)} %bitcast.32.len_ref, f32[448,768]{1,0:T(8,128)} %get-tuple-element.179.x3_ref, bf16[448,768]{1,0:T(8,128)(2,1)} %bitcast.170, ...), custom_call_target="tpu_custom_call" | custom-call | tf_op jit(solution)/shard_map/pallas_call | solution.py:426
  293.6 22.4 %shard_map.142 = (f32[448,768]{1,0:T(8,128)}, f32[448,768]{1,0:T(8,128)}, f32[5,768]{1,0:T(8,128)}, bf16[32,384,768]{2,1,0:T(8,128)(2,1)}) custom-call(s32[32]{0:T(128)} %fusion.23.slot_ref, f32[448,768]{1,0:T(8,128)} %get-tuple-element.182.dx3_ref, f32[448,768]{1,0:T(8,128)} %get-tuple-element.143.x2_ref, ...), custom_call_target="tpu_custom_call", output_to_operand_aliasing={{3}: (11, {})} | custom-call | tf_op jit(solution)/shard_map/pallas_call | solution.py:433
  316.0 22.8 %shard_map.143 = (f32[448,768]{1,0:T(8,128)}, f32[5,768]{1,0:T(8,128)}, bf16[32,384,768]{2,1,0:T(8,128)(2,1)}) custom-call(s32[32]{0:T(128)} %fusion.23.slot_ref, f32[448,768]{1,0:T(8,128)} %get-tuple-element.190.dx2_ref, bf16[448,768]{1,0:T(8,128)(2,1)} %bitcast.169, bf16[448,768]{1,0:T(8,128)(2,1)} %get-tuple-element.191.q_ref, ...), custom_call_target="tpu_custom_call", output_to_operand_aliasing={{2}: (10, {})} | custom-call | tf_op jit(solution)/shard_map/pallas_call | solution.py:441
  338.8 4.1 fusion.30
  366.2 10.4 %collective-permute-done.74 = bf16[384,768]{1,0:T(8,128)(2,1)S(1)} collective-permute-done((bf16[384,768]{1,0:T(8,128)(2,1)S(1)}, bf16[384,768]{1,0:T(8,128)(2,1)S(1)}, u32[]{:S(2)}, u32[]{:S(2)}) %collective-permute-start.74) | collective-permute-done | bytes 589856 | tf_op jit(solution)/shard_map/ppermute | solution.py:478
  382.2 8.2 %collective-permute-done.73 = bf16[384,768]{1,0:T(8,128)(2,1)S(1)} collective-permute-done((bf16[384,768]{1,0:T(8,128)(2,1)S(1)}, bf16[384,768]{1,0:T(8,128)(2,1)S(1)}, u32[]{:S(2)}, u32[]{:S(2)}) %collective-permute-start.73) | collective-permute-done | bytes 589856 | tf_op jit(solution)/shard_map/ppermute | solution.py:478
  404.3 3.9 collective-permute-done.79
  408.2 5.9 %collective-permute-done.80 = bf16[384,768]{1,0:T(8,128)(2,1)S(1)} collective-permute-done((bf16[384,768]{1,0:T(8,128)(2,1)S(1)}, bf16[384,768]{1,0:T(8,128)(2,1)S(1)}, u32[]{:S(2)}, u32[]{:S(2)}) %collective-permute-start.80) | collective-permute-done | bytes 589856 | tf_op jit(solution)/shard_map/ppermute | solution.py:481
  418.0 8.8 %collective-permute-done.84 = bf16[384,768]{1,0:T(8,128)(2,1)S(1)} collective-permute-done((bf16[384,768]{1,0:T(8,128)(2,1)S(1)}, bf16[384,768]{1,0:T(8,128)(2,1)S(1)}, u32[]{:S(2)}, u32[]{:S(2)}) %collective-permute-start.84) | collective-permute-done | bytes 589856 | tf_op jit(solution)/shard_map/ppermute | solution.py:481
  447.1 4.1 collective-permute-done.92
  452.0 5.2 %collective-permute-done.93 = f32[17,768]{1,0:T(8,128)} collective-permute-done((f32[17,768]{1,0:T(8,128)S(1)}, f32[17,768]{1,0:T(8,128)}, u32[]{:S(2)}, u32[]{:S(2)}) %collective-permute-start.93) | collective-permute-done | bytes 52256 | tf_op jit(solution)/shard_map/ppermute | solution.py:478
  (317 shorter events, 142.1 us)
Async XLA Ops:
  19.7 19.3 %collective-permute-start.12 = (bf16[288,768]{1,0:T(8,128)(2,1)S(1)}, bf16[288,768]{1,0:T(8,128)(2,1)S(1)}, u32[]{:S(2)}, u32[]{:S(2)}) collective-permute-start(bf16[288,768]{1,0:T(8,128)(2,1)S(1)} %collective-permute-done.8.refs_3_), channel_id=1, source_target_pairs={{0,4},{2,6},{4,0},{6,2},{8,12},{10,14},{12,8},{14,10},{16,20},{18,... | collective-permute-start | bytes 1327112 | tf_op jit(solution)/shard_map/ppermute | solution.py:481
  75.5 22.5 %collective-permute-start.39 = (bf16[384,768]{1,0:T(8,128)(2,1)}, bf16[384,768]{1,0:T(8,128)(2,1)S(1)}, u32[]{:S(2)}, u32[]{:S(2)}) collective-permute-start(bf16[384,768]{1,0:T(8,128)(2,1)} %refs_0_), channel_id=1, source_target_pairs={{0,8},{2,10},{4,12},{6,14},{8,16},{10,18},{12,20},{14,22},{16,24},... | collective-permute-start | bytes 1769480 | tf_op jit(solution)/shard_map/ppermute | solution.py:478
  98.0 28.8 %collective-permute-start.40 = (bf16[384,768]{1,0:T(8,128)(2,1)S(1)}, bf16[384,768]{1,0:T(8,128)(2,1)S(1)}, u32[]{:S(2)}, u32[]{:S(2)}) collective-permute-start(bf16[384,768]{1,0:T(8,128)(2,1)S(1)} %collective-permute-done.38.refs_2_), channel_id=1, source_target_pairs={{0,4},{2,6},{4,0},{6,2},{8,12},{10,14},{12,8},{14,10},{16,20},{18,... | collective-permute-start | bytes 1769480 | tf_op jit(solution)/shard_map/ppermute | solution.py:481
  99.0 27.8 %collective-permute-start.41 = (bf16[384,768]{1,0:T(8,128)(2,1)S(1)}, bf16[384,768]{1,0:T(8,128)(2,1)S(1)}, u32[]{:S(2)}, u32[]{:S(2)}) collective-permute-start(bf16[384,768]{1,0:T(8,128)(2,1)S(1)} %collective-permute-done.39.refs_3_), channel_id=1, source_target_pairs={{0,1},{1,0},{2,3},{3,2},{4,5},{5,4},{6,7},{7,6},{8,9},{9,8},{10,11... | collective-permute-start | bytes 1769480 | tf_op jit(solution)/shard_map/ppermute | solution.py:487
  100.7 26.1 %collective-permute-start.42 = (bf16[384,768]{1,0:T(8,128)(2,1)S(1)}, bf16[384,768]{1,0:T(8,128)(2,1)S(1)}, u32[]{:S(2)}, u32[]{:S(2)}) collective-permute-start(bf16[384,768]{1,0:T(8,128)(2,1)S(1)} %collective-permute-done.39.refs_3_), channel_id=1, source_target_pairs={{0,8},{2,10},{4,12},{6,14},{8,16},{10,18},{12,20},{14,22},{16,24},... | collective-permute-start | bytes 1769480 | tf_op jit(solution)/shard_map/ppermute | solution.py:478
  100.9 42.4 %collective-permute-start.43 = (bf16[384,768]{1,0:T(8,128)(2,1)S(1)}, bf16[384,768]{1,0:T(8,128)(2,1)S(1)}, u32[]{:S(2)}, u32[]{:S(2)}) collective-permute-start(bf16[384,768]{1,0:T(8,128)(2,1)S(1)} %collective-permute-done.39.refs_3_), channel_id=1, source_target_pairs={{0,4},{2,6},{4,0},{6,2},{8,12},{10,14},{12,8},{14,10},{16,20},{18,... | collective-permute-start | bytes 1769480 | tf_op jit(solution)/shard_map/ppermute | solution.py:481
  104.0 21.0 %collective-permute-start.1 = (bf16[2,696]{1,0:T(2,128)(2,1)S(1)}, bf16[2,696]{1,0:T(2,128)(2,1)S(1)}, u32[]{:S(2)}, u32[]{:S(2)}) collective-permute-start(bf16[2,696]{1,0:T(2,128)(2,1)S(1)} %pad_maximum_fusion.2), channel_id=1, source_target_pairs={{0,4},{2,6},{4,0},{6,2},{8,12},{10,14},{12,8},{14,10},{16,20},{18,... | collective-permute-start | bytes 8360 | tf_op jit(solution)/shard_map/ppermute | solution.py:481
  126.8 17.0 %collective-permute-start.44 = (bf16[384,768]{1,0:T(8,128)(2,1)S(1)}, bf16[384,768]{1,0:T(8,128)(2,1)}, u32[]{:S(2)}, u32[]{:S(2)}) collective-permute-start(bf16[384,768]{1,0:T(8,128)(2,1)S(1)} %collective-permute-done.42.refs_6_), channel_id=1, source_target_pairs={{0,1},{1,0},{2,3},{3,2},{4,5},{5,4},{6,7},{7,6},{8,9},{9,8},{10,11... | collective-permute-start | bytes 1769480 | tf_op jit(solution)/shard_map/ppermute | solution.py:487
  134.6 16.0 %collective-permute-start.52 = (bf16[384,768]{1,0:T(8,128)(2,1)}, bf16[384,768]{1,0:T(8,128)(2,1)S(1)}, u32[]{:S(2)}, u32[]{:S(2)}) collective-permute-start(bf16[384,768]{1,0:T(8,128)(2,1)} %refs_0_), channel_id=1, source_target_pairs={{0,2},{2,0},{4,6},{6,4},{8,10},{10,8},{12,14},{14,12},{16,18},{18,... | collective-permute-start | bytes 1769480 | tf_op jit(solution)/shard_map/ppermute | solution.py:484
  150.7 18.1 %collective-permute-start.48 = (bf16[384,768]{1,0:T(8,128)(2,1)S(1)}, bf16[384,768]{1,0:T(8,128)(2,1)S(1)}, u32[]{:S(2)}, u32[]{:S(2)}) collective-permute-start(bf16[384,768]{1,0:T(8,128)(2,1)S(1)} %collective-permute-done.40.refs_4_), channel_id=1, source_target_pairs={{0,8},{2,10},{4,12},{6,14},{8,16},{10,18},{12,20},{14,22},{16,24},... | collective-permute-start | bytes 1769480 | tf_op jit(solution)/shard_map/ppermute | solution.py:478
  150.7 27.1 %collective-permute-start.51 = (bf16[384,768]{1,0:T(8,128)(2,1)S(1)}, bf16[384,768]{1,0:T(8,128)(2,1)S(1)}, u32[]{:S(2)}, u32[]{:S(2)}) collective-permute-start(bf16[384,768]{1,0:T(8,128)(2,1)S(1)} %collective-permute-done.40.refs_4_), channel_id=1, source_target_pairs={{0,24},{2,26},{4,28},{6,30},{8,0},{10,2},{12,4},{14,6},{16,8},{18,... | collective-permute-start | bytes 1769480 | tf_op jit(solution)/shard_map/ppermute | solution.py:478
  154.6 23.9 %collective-permute-start.47 = (bf16[384,768]{1,0:T(8,128)(2,1)}, bf16[384,768]{1,0:T(8,128)(2,1)}, u32[]{:S(2)}, u32[]{:S(2)}) collective-permute-start(bf16[384,768]{1,0:T(8,128)(2,1)} %collective-permute-done.45.refs_9_), channel_id=1, source_target_pairs={{0,1},{1,0},{2,3},{3,2},{4,5},{5,4},{6,7},{7,6},{8,9},{9,8},{10,11... | collective-permute-start | bytes 1769480 | tf_op jit(solution)/shard_map/ppermute | solution.py:487
  156.0 22.6 %collective-permute-start.56 = (bf16[384,768]{1,0:T(8,128)(2,1)S(1)}, bf16[384,768]{1,0:T(8,128)(2,1)S(1)}, u32[]{:S(2)}, u32[]{:S(2)}) collective-permute-start(bf16[384,768]{1,0:T(8,128)(2,1)S(1)} %collective-permute-done.40.refs_4_), channel_id=1, source_target_pairs={{0,2},{2,0},{4,6},{6,4},{8,10},{10,8},{12,14},{14,12},{16,18},{18,... | collective-permute-start | bytes 1769480 | tf_op jit(solution)/shard_map/ppermute | solution.py:484
  164.0 16.3 %collective-permute-start.57 = (bf16[384,768]{1,0:T(8,128)(2,1)S(1)}, bf16[384,768]{1,0:T(8,128)(2,1)S(1)}, u32[]{:S(2)}, u32[]{:S(2)}) collective-permute-start(bf16[384,768]{1,0:T(8,128)(2,1)S(1)} %collective-permute-done.41.refs_5_), channel_id=1, source_target_pairs={{0,2},{2,0},{4,6},{6,4},{8,10},{10,8},{12,14},{14,12},{16,18},{18,... | collective-permute-start | bytes 1769480 | tf_op jit(solution)/shard_map/ppermute | solution.py:484
  178.6 44.6 %collective-permute-start.50 = (bf16[384,768]{1,0:T(8,128)(2,1)}, bf16[384,768]{1,0:T(8,128)(2,1)}, u32[]{:S(2)}, u32[]{:S(2)}) collective-permute-start(bf16[384,768]{1,0:T(8,128)(2,1)} %collective-permute-done.46.refs_10_), channel_id=1, source_target_pairs={{0,1},{1,0},{2,3},{3,2},{4,5},{5,4},{6,7},{7,6},{8,9},{9,8},{10,11... | collective-permute-start | bytes 1769480 | tf_op jit(solution)/shard_map/ppermute | solution.py:487
  180.3 44.2 %collective-permute-start.60 = (bf16[384,768]{1,0:T(8,128)(2,1)}, bf16[384,768]{1,0:T(8,128)(2,1)}, u32[]{:S(2)}, u32[]{:S(2)}) collective-permute-start(bf16[384,768]{1,0:T(8,128)(2,1)} %collective-permute-done.44.refs_8_), channel_id=1, source_target_pairs={{0,2},{2,0},{4,6},{6,4},{8,10},{10,8},{12,14},{14,12},{16,18},{18,... | collective-permute-start | bytes 1769480 | tf_op jit(solution)/shard_map/ppermute | solution.py:484
  180.6 43.9 %collective-permute-start.61 = (bf16[384,768]{1,0:T(8,128)(2,1)}, bf16[384,768]{1,0:T(8,128)(2,1)}, u32[]{:S(2)}, u32[]{:S(2)}) collective-permute-start(bf16[384,768]{1,0:T(8,128)(2,1)} %collective-permute-done.45.refs_9_), channel_id=1, source_target_pairs={{0,2},{2,0},{4,6},{6,4},{8,10},{10,8},{12,14},{14,12},{16,18},{18,... | collective-permute-start | bytes 1769480 | tf_op jit(solution)/shard_map/ppermute | solution.py:484
  191.6 33.4 %collective-permute-start.62 = (bf16[384,768]{1,0:T(8,128)(2,1)}, bf16[384,768]{1,0:T(8,128)(2,1)}, u32[]{:S(2)}, u32[]{:S(2)}) collective-permute-start(bf16[384,768]{1,0:T(8,128)(2,1)} %collective-permute-done.46.refs_10_), channel_id=1, source_target_pairs={{0,2},{2,0},{4,6},{6,4},{8,10},{10,8},{12,14},{14,12},{16,18},{18,... | collective-permute-start | bytes 1769480 | tf_op jit(solution)/shard_map/ppermute | solution.py:484
  191.7 33.5 %collective-permute-start.63 = (bf16[384,768]{1,0:T(8,128)(2,1)}, bf16[384,768]{1,0:T(8,128)(2,1)}, u32[]{:S(2)}, u32[]{:S(2)}) collective-permute-start(bf16[384,768]{1,0:T(8,128)(2,1)} %collective-permute-done.47.refs_11_), channel_id=1, source_target_pairs={{0,2},{2,0},{4,6},{6,4},{8,10},{10,8},{12,14},{14,12},{16,18},{18,... | collective-permute-start | bytes 1769480 | tf_op jit(solution)/shard_map/ppermute | solution.py:484
  223.2 28.1 %collective-permute-start.68 = (bf16[448,768]{1,0:T(8,128)(2,1)}, bf16[448,768]{1,0:T(8,128)(2,1)S(1)}, u32[]{:S(2)}, u32[]{:S(2)}) collective-permute-start(bf16[448,768]{1,0:T(8,128)(2,1)} %shard_map.139.mine_ref), channel_id=1, source_target_pairs={{0,1},{1,0},{2,3},{3,2},{4,5},{5,4},{6,7},{7,6},{8,9},{9,8},{10,11... | collective-permute-start | bytes 2064392 | tf_op jit(solution)/shard_map/ppermute | solution.py:487
  360.9 15.7 %collective-permute-start.74 = (bf16[384,768]{1,0:T(8,128)(2,1)S(1)}, bf16[384,768]{1,0:T(8,128)(2,1)S(1)}, u32[]{:S(2)}, u32[]{:S(2)}) collective-permute-start(bf16[384,768]{1,0:T(8,128)(2,1)S(1)} %get-tuple-element.240), channel_id=1, source_target_pairs={{0,24},{2,26},{4,28},{6,30},{8,0},{10,2},{12,4},{14,6},{16,8},{18,... | collective-permute-start | bytes 1769480 | tf_op jit(solution)/shard_map/ppermute | solution.py:478
  362.8 16.2 %collective-permute-start.75 = (bf16[384,768]{1,0:T(8,128)(2,1)S(1)}, bf16[384,768]{1,0:T(8,128)(2,1)S(1)}, u32[]{:S(2)}, u32[]{:S(2)}) collective-permute-start(bf16[384,768]{1,0:T(8,128)(2,1)S(1)} %get-tuple-element.241), channel_id=1, source_target_pairs={{0,1},{1,0},{2,3},{3,2},{4,5},{5,4},{6,7},{7,6},{8,9},{9,8},{10,11... | collective-permute-start | bytes 1769480 | tf_op jit(solution)/shard_map/ppermute | solution.py:487
  364.3 26.1 %collective-permute-start.73 = (bf16[384,768]{1,0:T(8,128)(2,1)S(1)}, bf16[384,768]{1,0:T(8,128)(2,1)S(1)}, u32[]{:S(2)}, u32[]{:S(2)}) collective-permute-start(bf16[384,768]{1,0:T(8,128)(2,1)S(1)} %get-tuple-element.239), channel_id=1, source_target_pairs={{0,8},{2,10},{4,12},{6,14},{8,16},{10,18},{12,20},{14,22},{16,24},... | collective-permute-start | bytes 1769480 | tf_op jit(solution)/shard_map/ppermute | solution.py:478
  364.5 27.2 %collective-permute-start.78 = (bf16[384,768]{1,0:T(8,128)(2,1)S(1)}, bf16[384,768]{1,0:T(8,128)(2,1)S(1)}, u32[]{:S(2)}, u32[]{:S(2)}) collective-permute-start(bf16[384,768]{1,0:T(8,128)(2,1)S(1)} %get-tuple-element.238), channel_id=1, source_target_pairs={{0,1},{1,0},{2,3},{3,2},{4,5},{5,4},{6,7},{7,6},{8,9},{9,8},{10,11... | collective-permute-start | bytes 1769480 | tf_op jit(solution)/shard_map/ppermute | solution.py:487
  381.6 22.7 %collective-permute-start.82 = (bf16[384,768]{1,0:T(8,128)(2,1)S(1)}, bf16[384,768]{1,0:T(8,128)(2,1)S(1)}, u32[]{:S(2)}, u32[]{:S(2)}) collective-permute-start(bf16[384,768]{1,0:T(8,128)(2,1)S(1)} %get-tuple-element.226), channel_id=1, source_target_pairs={{0,1},{1,0},{2,3},{3,2},{4,5},{5,4},{6,7},{7,6},{8,9},{9,8},{10,11... | collective-permute-start | bytes 1769480 | tf_op jit(solution)/shard_map/ppermute | solution.py:487
  397.9 16.3 %collective-permute-start.80 = (bf16[384,768]{1,0:T(8,128)(2,1)S(1)}, bf16[384,768]{1,0:T(8,128)(2,1)S(1)}, u32[]{:S(2)}, u32[]{:S(2)}) collective-permute-start(bf16[384,768]{1,0:T(8,128)(2,1)S(1)} %get-tuple-element.227), channel_id=1, source_target_pairs={{0,4},{2,6},{4,0},{6,2},{8,12},{10,14},{12,8},{14,10},{16,20},{18,... | collective-permute-start | bytes 1769480 | tf_op jit(solution)/shard_map/ppermute | solution.py:481
  399.1 27.7 %collective-permute-start.84 = (bf16[384,768]{1,0:T(8,128)(2,1)S(1)}, bf16[384,768]{1,0:T(8,128)(2,1)S(1)}, u32[]{:S(2)}, u32[]{:S(2)}) collective-permute-start(bf16[384,768]{1,0:T(8,128)(2,1)S(1)} %get-tuple-element.225), channel_id=1, source_target_pairs={{0,4},{2,6},{4,0},{6,2},{8,12},{10,14},{12,8},{14,10},{16,20},{18,... | collective-permute-start | bytes 1769480 | tf_op jit(solution)/shard_map/ppermute | solution.py:481
  399.9 26.9 %collective-permute-start.85 = (bf16[384,768]{1,0:T(8,128)(2,1)S(1)}, bf16[384,768]{1,0:T(8,128)(2,1)S(1)}, u32[]{:S(2)}, u32[]{:S(2)}) collective-permute-start(bf16[384,768]{1,0:T(8,128)(2,1)S(1)} %get-tuple-element.224), channel_id=1, source_target_pairs={{0,1},{1,0},{2,3},{3,2},{4,5},{5,4},{6,7},{7,6},{8,9},{9,8},{10,11... | collective-permute-start | bytes 1769480 | tf_op jit(solution)/shard_map/ppermute | solution.py:487
  415.7 43.0 %collective-permute-start.69 = (bf16[448,768]{1,0:T(8,128)(2,1)S(1)}, bf16[448,768]{1,0:T(8,128)(2,1)S(1)}, u32[]{:S(2)}, u32[]{:S(2)}) collective-permute-start(bf16[448,768]{1,0:T(8,128)(2,1)S(1)} %convert_element_type.257), channel_id=1, source_target_pairs={{0,1},{1,0},{2,3},{3,2},{4,5},{5,4},{6,7},{7,6},{8,9},{9,8},{10,11... | collective-permute-start | bytes 2064392 | tf_op jit(solution)/shard_map/ppermute | solution.py:487
  416.8 43.2 %collective-permute-start.87 = (bf16[384,768]{1,0:T(8,128)(2,1)S(1)}, bf16[384,768]{1,0:T(8,128)(2,1)}, u32[]{:S(2)}, u32[]{:S(2)}) collective-permute-start(bf16[384,768]{1,0:T(8,128)(2,1)S(1)} %get-tuple-element.233), channel_id=1, source_target_pairs={{0,4},{2,6},{4,0},{6,2},{8,12},{10,14},{12,8},{14,10},{16,20},{18,... | collective-permute-start | bytes 1769480 | tf_op jit(solution)/shard_map/ppermute | solution.py:481
  433.4 26.6 %collective-permute-start.86 = (bf16[384,768]{1,0:T(8,128)(2,1)}, bf16[384,768]{1,0:T(8,128)(2,1)}, u32[]{:S(2)}, u32[]{:S(2)}) collective-permute-start(bf16[384,768]{1,0:T(8,128)(2,1)} %get-tuple-element.223), channel_id=1, source_target_pairs={{0,24},{2,26},{4,28},{6,30},{8,0},{10,2},{12,4},{14,6},{16,8},{18,... | collective-permute-start | bytes 1769480 | tf_op jit(solution)/shard_map/ppermute | solution.py:478
  433.4 26.6 %collective-permute-start.88 = (bf16[384,768]{1,0:T(8,128)(2,1)}, bf16[384,768]{1,0:T(8,128)(2,1)}, u32[]{:S(2)}, u32[]{:S(2)}) collective-permute-start(bf16[384,768]{1,0:T(8,128)(2,1)} %get-tuple-element.222), channel_id=1, source_target_pairs={{0,1},{1,0},{2,3},{3,2},{4,5},{5,4},{6,7},{7,6},{8,9},{9,8},{10,11... | collective-permute-start | bytes 1769480 | tf_op jit(solution)/shard_map/ppermute | solution.py:487
  (118 other events, 2970.6 us)
